TPU v7x, 512 devices: a whole 4x8x8 slice. The times are simulated.
512 devices in a mesh: row: 32 (over y, x), col: 16 (over z, core).
Axes of the slice: x: 4, y: 8, z: 8, core: 2. Of those that a mesh axis runs over, the one named last changes fastest.
Arguments:
- tokens: int32 [256], replicated, may hold values from 0 to 8191
- emission_table: bfloat16 [8192, 32768], P('row', 'col'), may hold values from -3 to 0
- forward_rows: bfloat16 [256, 32768], P('col', 'row'), may hold values from 0.05 to 64
- backward_rows: bfloat16 [256, 32768], P('row', 'col'), may hold values from 0.05 to 64
- src_embed: bfloat16 [32768, 256], P(('row', 'col')), may hold values from -12 to 12
- tgt_embed: bfloat16 [32768, 256], P(('col', 'row')), may hold values from -12 to 12
Outputs:
- grad_src: float32 [32768, 256], P(('row', 'col'))
- grad_tgt: float32 [32768, 256], P(('col', 'row'))
All inputs are finite; a program needn't handle non-finite values.
Results may differ from a plain program's by a relative error of at most 0.018.
Values may be sent and summed in bfloat16 or wider, within the bound.
No kernel may reach another device: no remote copies, remote signals or barrier semaphores. Data moves between devices by JAX's collectives and lax.ppermute only.
A program may use at most 64 MiB of HBM per device.

v0:
```python
import jax
import jax.numpy as jnp
from jax import lax
from jax.sharding import PartitionSpec as P

S = 32768
SEQS = 256


def on_device(tokens, emission_table, forward_rows, backward_rows, src_embed, tgt_embed):
    src_block = lax.all_gather(src_embed, "col", axis=0, tiled=True)
    tgt_block = lax.all_gather(tgt_embed, "row", axis=0, tiled=True)
    forward_all = lax.all_gather(forward_rows, "col", axis=0, tiled=True).astype(jnp.float32)
    logits = lax.dot_general(
        src_block, tgt_block, (((1,), (1,)), ((), ())), preferred_element_type=jnp.float32
    )
    row_peak = lax.pmax(jnp.max(logits, axis=1), "col")
    exp_full = jnp.exp(logits - row_peak[:, None])
    local_sums = jnp.sum(exp_full, axis=1)
    exp_block = exp_full.astype(jnp.bfloat16)
    vocab_local = emission_table.shape[0]
    offset = lax.axis_index("row") * vocab_local
    onehot = (tokens[:, None] == offset + jnp.arange(vocab_local, dtype=jnp.int32)[None, :]).astype(
        jnp.bfloat16
    )
    looked = jnp.dot(onehot, emission_table, preferred_element_type=jnp.float32)
    summed_looks = lax.psum(looked.astype(jnp.bfloat16), "row").astype(jnp.float32)
    backward_all = lax.all_gather(backward_rows, "row", axis=0, tiled=True)
    weighted = (jnp.exp(summed_looks) * backward_all.astype(jnp.float32)).astype(jnp.bfloat16)
    local_reach = lax.dot_general(
        weighted, exp_block, (((1,), (1,)), ((), ())), preferred_element_type=jnp.float32
    )
    row_sums, reach = lax.psum((local_sums, local_reach), "col")
    local_norm = jnp.sum(forward_all * reach / row_sums[None, :], axis=1)
    norm_terms = lax.psum(local_norm, "row")
    factor = jnp.float32(S) / jnp.float32(SEQS)
    coeffs = (factor * forward_all / (norm_terms[:, None] * row_sums[None, :])).astype(jnp.bfloat16)
    summed = lax.dot_general(
        coeffs, weighted, (((0,), (0,)), ((), ())), preferred_element_type=jnp.float32
    )
    exp_wide = exp_block.astype(jnp.float32)
    counts = exp_wide * summed
    row_counts = lax.psum(jnp.sum(counts, axis=1), "col")
    grad_logits = (counts - exp_wide * (row_counts / row_sums)[:, None]).astype(jnp.bfloat16)
    piece = grad_logits
    grad_src = lax.psum_scatter(
        jnp.dot(piece, tgt_block, preferred_element_type=jnp.float32),
        "col",
        scatter_dimension=0,
        tiled=True,
    )
    piece = grad_logits
    grad_tgt = lax.psum_scatter(
        lax.dot_general(
            piece, src_block, (((0,), (0,)), ((), ())), preferred_element_type=jnp.float32
        ),
        "row",
        scatter_dimension=0,
        tiled=True,
    )
    return (grad_src, grad_tgt)


def solution(mesh):
    in_specs = (
        P(),
        P("row", "col"),
        P("col", "row"),
        P("row", "col"),
        P(("row", "col"), None),
        P(("col", "row"), None),
    )
    out_specs = (P(("row", "col"), None), P(("col", "row"), None))
    return jax.shard_map(
        on_device, mesh=mesh, in_specs=in_specs, out_specs=out_specs, check_vma=False
    )
```

profile of v0, /device:TPU:1, one launch (start us, length us, event | category | flops | bytes accessed | tf_op | source)
XLA Modules:
  0.0 861.8 jit_solution(17556613860156256571)
XLA Ops:
  7.2 0.0 copy-start
  7.2 0.0 all-gather.3.cloned.1.call-start
  7.2 0.7 all-gather.3.cloned.1.call-update
  7.9 0.0 all-reduce.3.cloned.1.call-start
  8.0 0.4 copy-done
  8.4 2.2 convolution_convert_fusion
  10.5 0.0 all-reduce.3.cloned.1.call-update
  10.6 0.0 all-gather.5.cloned.1.call-start
  10.6 0.7 all-gather.5.cloned.1.call-update
  11.3 0.0 all-reduce.5.cloned.1.call-start
  11.4 26.2 %all_gather.12 = bf16[1024,256]{1,0:T(8,128)(2,1)S(1)} all-gather(bf16[64,256]{1,0:T(8,128)(2,1)} %param.10), channel_id=1, replica_groups=mesh['row'=32,'col'=16] {'col'}, dimensions={0}, use_global_device_ids=true | all-gather | bytes 557056 | tf_op jit(solution)/shard_map/all_gather | solution.py:11
  37.5 56.2 %all-gather.3.cloned.1.call-done = bf16[2048,256]{1,0:T(8,128)(2,1)} async-done(((bf16[64,256]{1,0:T(8,128)(2,1)}), bf16[2048,256]{1,0:T(8,128)(2,1)}) %all-gather.3.cloned.1.call-update) | async-done | bytes 1048592 | tf_op jit(solution)/shard_map/all_gather | solution.py:12
  93.7 5.7 fusion.19
  99.5 29.7 %pmax.7 = f32[1024]{0:T(1024)S(1)} all-reduce(f32[1024]{0:T(1024)S(1)} %get-tuple-element.4), channel_id=1, replica_groups=mesh['row'=32,'col'=16] {'col'}, use_global_device_ids=true, to_apply=%region_1.0 | all-reduce | flops 1024 | bytes 8192 | tf_op jit(solution)/shard_map/pmax | solution.py:17
  129.2 5.6 fusion.2
  134.8 120.8 %all-reduce.3.cloned.1.call-done = bf16[256,2048]{1,0:T(8,128)(2,1)} async-done(((bf16[256,2048]{1,0:T(8,128)(2,1)}), bf16[256,2048]{1,0:T(8,128)(2,1)}) %all-reduce.3.cloned.1.call-update) | async-done | bytes 1048592 | tf_op jit(solution)/shard_map/psum | solution.py:27
  255.5 82.4 %all-gather.5.cloned.1.call-done = bf16[256,2048]{1,0:T(8,128)(2,1)} async-done(((bf16[8,2048]{1,0:T(8,128)(2,1)}), bf16[256,2048]{1,0:T(8,128)(2,1)}) %all-gather.5.cloned.1.call-update) | async-done | bytes 1048592 | tf_op jit(solution)/shard_map/all_gather | solution.py:28
  338.0 0.0 copy-start.4
  338.0 0.0 copy-start.3
  338.0 5.2 fusion.14
  343.2 0.0 all-reduce.5.cloned.1.call-update
  343.2 0.0 reduce-scatter.3.cloned.1.call-start
  343.3 0.0 copy-done.4
  343.3 24.6 %all_gather.14 = bf16[256,1024]{1,0:T(8,128)(2,1)S(1)} all-gather(bf16[16,1024]{1,0:T(8,128)(2,1)S(1)} %copy-done.4), channel_id=1, replica_groups=mesh['row'=32,'col'=16] {'col'}, dimensions={0}, use_global_device_ids=true | all-gather | bytes 557056 | tf_op jit(solution)/shard_map/all_gather | solution.py:13
  367.9 23.0 %psum.37 = f32[1024]{0:T(1024)S(1)} all-reduce(f32[1024]{0:T(1024)S(1)} %get-tuple-element.2), channel_id=1, replica_groups=mesh['row'=32,'col'=16] {'col'}, use_global_device_ids=true, to_apply=%region_5.0 | all-reduce | flops 1024 | bytes 8192 | tf_op jit(solution)/shard_map/psum | solution.py:33
  390.9 72.3 %all-reduce.5.cloned.1.call-done = f32[256,1024]{1,0:T(8,128)} async-done(((f32[256,1024]{1,0:T(8,128)}), f32[256,1024]{1,0:T(8,128)}) %all-reduce.5.cloned.1.call-update) | async-done | bytes 1048592 | tf_op jit(solution)/shard_map/psum | solution.py:33
  463.2 1.4 fusion.8
  464.7 60.4 %psum.38 = f32[256]{0:T(256)S(1)} all-reduce(f32[256]{0:T(256)S(1)} %fusion.8), channel_id=1, replica_groups=mesh['row'=32,'col'=16] {'row'}, use_global_device_ids=true, to_apply=%region_7.0 | all-reduce | flops 256 | bytes 2048 | tf_op jit(solution)/shard_map/psum | solution.py:35
  525.1 0.0 copy-done.3
  525.1 7.3 fusion.4
  532.4 37.9 %psum.39 = f32[1024]{0:T(1024)S(1)} all-reduce(f32[1024]{0:T(1024)S(1)} %get-tuple-element.6), channel_id=1, replica_groups=mesh['row'=32,'col'=16] {'col'}, use_global_device_ids=true, to_apply=%region_9.0 | all-reduce | flops 1024 | bytes 8192 | tf_op jit(solution)/shard_map/psum | solution.py:43
  570.3 0.0 copy-start.2
  570.3 5.5 fusion.1
  575.8 0.0 copy-start.1
  575.8 1.9 copy-done.1
  577.7 0.0 copy-done.2
  577.7 2.3 fusion.20
  580.0 0.0 reduce-scatter.3.cloned.1.call-update
  580.0 0.0 reduce-scatter.5.cloned.1.call-start
  580.0 4.8 fusion.21
  584.9 0.0 reduce-scatter.5.cloned.1.call-update
  584.9 48.2 %reduce-scatter.3.cloned.1.call-done = f32[64,256]{1,0:T(8,128)} async-done(((f32[1024,256]{1,0:T(8,128)}), f32[64,256]{1,0:T(8,128)}) %reduce-scatter.3.cloned.1.call-update) | async-done | bytes 65552 | tf_op jit(solution)/shard_map/reduce_scatter | solution.py:46
  633.1 221.8 %reduce-scatter.5.cloned.1.call-done = f32[64,256]{1,0:T(8,128)} async-done(((f32[2048,256]{1,0:T(8,128)}), f32[64,256]{1,0:T(8,128)}) %reduce-scatter.5.cloned.1.call-update) | async-done | bytes 65552 | tf_op jit(solution)/shard_map/reduce_scatter | solution.py:53
  (2 shorter events, 0.0 us)
Async XLA Ops:
  7.2 1.2 copy-start
  7.2 86.6 %all-gather.3.cloned.1.call-start = ((), (), s32[]{:S(2)}) async-start(), calls=%async_computation.2 | async-start | bytes 1081344 | tf_op jit(solution)/shard_map/all_gather | solution.py:12
  7.9 247.6 %all-reduce.3.cloned.1.call-start = ((), (), s32[]{:S(2)}) async-start(), calls=%async_computation.3 | async-start | bytes 2097152 | tf_op jit(solution)/shard_map/psum | solution.py:27
  10.6 327.4 %all-gather.5.cloned.1.call-start = ((), (), s32[]{:S(2)}) async-start(), calls=%async_computation.4 | async-start | bytes 1081344 | tf_op jit(solution)/shard_map/all_gather | solution.py:28
  11.3 451.9 %all-reduce.5.cloned.1.call-start = ((), (), s32[]{:S(2)}) async-start(), calls=%async_computation.5 | async-start | bytes 2097152 | tf_op jit(solution)/shard_map/psum | solution.py:33
  338.0 5.3 copy-start.4
  338.0 187.1 %copy-start.3 = (bf16[256,2048]{1,0:T(8,128)(2,1)S(1)}, bf16[256,2048]{1,0:T(8,128)(2,1)}, u32[]{:S(2)}) copy-start(bf16[256,2048]{1,0:T(8,128)(2,1)} %all-reduce.3.cloned.1.call-done) | copy-start | bytes 3145732
  343.2 289.8 %reduce-scatter.3.cloned.1.call-start = ((), (), s32[]{:S(2)}) async-start(), calls=%async_computation.6 | async-start | bytes 1114112 | tf_op jit(solution)/shard_map/reduce_scatter | solution.py:46
  570.3 7.4 copy-start.2
  575.8 1.9 copy-start.1
  580.0 274.9 %reduce-scatter.5.cloned.1.call-start = ((), (), s32[]{:S(2)}) async-start(), calls=%async_computation.7 | async-start | bytes 2162688 | tf_op jit(solution)/shard_map/reduce_scatter | solution.py:53
Sparse Core Ops, SparseCore 0:
  11.2 82.5 all-gather.2
  97.2 158.3 all-reduce.2
  258.7 79.2 all-gather.4
  343.4 119.8 all-reduce.4
  580.1 52.8 reduce-scatter.2
  637.9 216.9 reduce-scatter.4
where the time goes:
time: 866 us; the launch traced here: 862 us
  waiting for transfers between devices  603 us (70%)
  blocking collectives  202 us (23%)
  matrix products  27.5 us (3%)
  between operations  14.2 us (2%)
  other arithmetic  12.5 us (1%)
    reduce_scatter x1, waiting for transfers between devices, on_device(): lax.psum_scatter(lax.dot_general(piece, src_block, (((0,), (0,)), ((), ()...  222 us
    psum x1, waiting for transfers between devices, on_device(): lax.psum(looked.astype(jnp.bfloat16), 'row').astype(jnp.float32)  121 us
    all_gather x1, waiting for transfers between devices, on_device(): backward_all = lax.all_gather(backward_rows, 'row', axis=0, tiled=True)  82.4 us
    psum x1, waiting for transfers between devices, on_device(): row_sums, reach = lax.psum((local_sums, local_reach), 'col')  72.3 us
    psum x1, blocking collectives, on_device(): norm_terms = lax.psum(local_norm, 'row')  60.4 us
    all_gather x1, waiting for transfers between devices, on_device(): tgt_block = lax.all_gather(tgt_embed, 'row', axis=0, tiled=True)  56.2 us
    reduce_scatter x1, waiting for transfers between devices, on_device(): lax.psum_scatter(jnp.dot(piece, tgt_block, preferred_element_type=jnp.flo...  48.2 us
    psum x1, blocking collectives, on_device(): row_counts = lax.psum(jnp.sum(counts, axis=1), 'col')  37.9 us
  transfers between devices with their start and end apart: 6, of which 6 were waited for; matrix products, arithmetic and copies ran while one was open for 2% of the time, Pallas kernels for 0%

commit v1 on v0

v1 whole, which is shorter than its diff:
```python
import jax
import jax.numpy as jnp
from jax import lax
from jax.sharding import PartitionSpec as P

S = 32768
SEQS = 256
ROWS = 32
COLS = 16
BF = jnp.bfloat16
F32 = jnp.float32


def gather_by(x, axis, n):
    return lax.all_to_all(jnp.broadcast_to(x[None], (n,) + x.shape), axis, 0, 0)


def halving_sum(parts):
    me = lax.axis_index("col")
    held = parts
    for bit in range(4):
        pairs = held.reshape((held.shape[0] // 2, 2) + held.shape[1:])
        mine = (me >> bit) & 1
        kept = jnp.where(mine == 0, pairs[:, 0], pairs[:, 1])
        sent = jnp.where(mine == 0, pairs[:, 1], pairs[:, 0]).astype(BF)
        got = lax.ppermute(sent, "col", [(k, k ^ (1 << bit)) for k in range(COLS)])
        held = kept + got.astype(F32)
    return held[0]


def on_device(tokens, emission_table, forward_rows, backward_rows, src_embed, tgt_embed):
    vocab_local = emission_table.shape[0]
    offset = lax.axis_index("row") * vocab_local
    onehot = (tokens[:, None] == offset + jnp.arange(vocab_local, dtype=jnp.int32)[None, :]).astype(BF)
    looked = jnp.dot(onehot, emission_table, preferred_element_type=F32).astype(BF)
    width = tgt_embed.shape[1]
    own = SEQS // ROWS
    looked = looked.reshape(ROWS, own, -1, width).transpose(0, 2, 1, 3).reshape(ROWS, -1, width)
    depth = looked.shape[1]
    sent = jnp.concatenate([looked, jnp.broadcast_to(tgt_embed[None], (ROWS,) + tgt_embed.shape)], axis=1)
    both = lax.all_to_all(sent, "row", 0, 0)
    tgt_block = both[:, depth:].reshape(-1, width)
    own_look = jnp.sum(both[:, :depth].astype(F32), axis=0)
    own_look = own_look.reshape(-1, own, width).transpose(1, 0, 2).reshape(own, -1)
    own_weighted = (jnp.exp(own_look) * backward_rows.astype(F32)).astype(BF)

    src_block = lax.all_gather(src_embed, "col", axis=0, tiled=True)
    forward_all = lax.all_gather(forward_rows, "col", axis=0, tiled=True)
    own_weighted, src_block, forward_all = lax.optimization_barrier((own_weighted, src_block, forward_all))
    weighted = gather_by(own_weighted, "row", ROWS).reshape(SEQS, -1)

    logits = lax.dot_general(src_block, tgt_block, (((1,), (1,)), ((), ())), preferred_element_type=F32)
    local_peak = jnp.max(logits, axis=1)
    exp_full = jnp.exp(logits - local_peak[:, None])
    local_sums = jnp.sum(exp_full, axis=1)
    exp_block = exp_full.astype(BF)

    peaks_sums = lax.all_gather(jnp.stack([local_peak, local_sums]), "col")
    row_peak = jnp.max(peaks_sums[:, 0], axis=0)
    row_sums = jnp.sum(peaks_sums[:, 1] * jnp.exp(peaks_sums[:, 0] - row_peak[None]), axis=0)
    scale = jnp.exp(local_peak - row_peak)

    reach = lax.dot_general(weighted, exp_block, (((1,), (1,)), ((), ())), preferred_element_type=F32)
    share = reach * (scale / row_sums)[None, :]
    norm_terms = jnp.sum(forward_all.astype(F32) * share, axis=1)
    norm_terms = jnp.sum(gather_by(norm_terms, "col", COLS), axis=0)
    norm_terms = jnp.sum(gather_by(norm_terms, "row", ROWS), axis=0)
    forward_all = forward_all.astype(F32)
    factor = jnp.float32(S) / jnp.float32(SEQS)
    coeffs = (factor * forward_all / (norm_terms[:, None] * row_sums[None, :])).astype(BF)
    part = jnp.sum(coeffs.astype(F32) * share, axis=0)
    ratio = jnp.sum(gather_by(part, "col", COLS), axis=0)

    summed = lax.dot_general(coeffs, weighted, (((0,), (0,)), ((), ())), preferred_element_type=F32)
    grad_logits = (exp_block.astype(F32) * scale[:, None] * (summed - ratio[:, None])).astype(BF)
    tgt_part = lax.dot_general(grad_logits, src_block, (((0,), (0,)), ((), ())), preferred_element_type=F32)
    tgt_parts = lax.all_to_all(tgt_part.astype(BF).reshape((ROWS,) + tgt_embed.shape), "row", 0, 0)
    src_part = jnp.dot(grad_logits, tgt_block, preferred_element_type=F32)
    grad_src = halving_sum(src_part.reshape((COLS,) + src_embed.shape))
    grad_tgt = jnp.sum(tgt_parts.astype(F32), axis=0)
    return (grad_src, grad_tgt)


def solution(mesh):
    in_specs = (
        P(),
        P("row", "col"),
        P("col", "row"),
        P("row", "col"),
        P(("row", "col"), None),
        P(("col", "row"), None),
    )
    out_specs = (P(("row", "col"), None), P(("col", "row"), None))
    return jax.shard_map(
        on_device, mesh=mesh, in_specs=in_specs, out_specs=out_specs, check_vma=False
    )
```

time: 866 us -> 198 us (0.23)
  waiting for transfers between devices: 603 us -> 29.9 us
  blocking collectives: 202 us -> 97.9 us
  starting transfers between devices: 0.24 us -> 35.9 us
  between operations: 14.2 us -> 0.99 us
  matrix products: 27.5 us -> 18.3 us
    reduce_scatter x2 -> x0, waiting for transfers between devices: 270 us -> none  [the longest x1 222 us: on_device(): lax.psum_scatter(lax.dot_general(piece, src_block, (((0,), (0,)), ((), ()...]
    psum x2 -> x0, waiting for transfers between devices: 193 us -> none  [the longest x1 121 us: on_device(): lax.psum(looked.astype(jnp.bfloat16), 'row').astype(jnp.float32)]
    all_gather x2 -> x0, waiting for transfers between devices: 139 us -> none  [the longest x1 82.4 us: on_device(): backward_all = lax.all_gather(backward_rows, 'row', axis=0, tiled=True)]
    psum x3 -> x0, blocking collectives: 121 us -> none  [the longest x1 60.4 us: on_device(): norm_terms = lax.psum(local_norm, 'row')]
    pmax x1 -> x0, blocking collectives: 29.7 us -> none  [on_device(): row_peak = lax.pmax(jnp.max(logits, axis=1), 'col')]
    all_to_all x0 -> x2, blocking collectives: none -> 28.6 us  [gather_by(): return lax.all_to_all(jnp.broadcast_to(x[None], (n,) + x.shape), axis, 0, 0)]
    all_to_all x0 -> x4, starting transfers between devices: none -> 26.4 us  [the longest x2 11.8 us: gather_by(): return lax.all_to_all(jnp.broadcast_to(x[None], (n,) + x.shape), axis, 0, 0)]
    all_gather x1 -> x2, blocking collectives: 24.6 us -> 42.6 us  [the longest x1 25.3 us: on_device(): peaks_sums = lax.all_gather(jnp.stack([local_peak, local_sums]), 'col')]
  transfers between devices with their start and end apart: 6 -> 8, of which waited for: 6 -> 6; matrix products, arithmetic and copies ran while one was open for 2% -> 4% of each run, Pallas kernels for 0% -> 0%
where the time goes in v1:
time: 198 us; the launch traced here: 197 us
  blocking collectives  97.9 us (49%)
  starting transfers between devices  35.9 us (18%)
  waiting for transfers between devices  29.9 us (15%)
  matrix products  18.3 us (9%)
  local copies, waits for them, and re-layouts  6.94 us (4%)
  other arithmetic  6.52 us (3%)
    all_to_all x2, blocking collectives, gather_by(): return lax.all_to_all(jnp.broadcast_to(x[None], (n,) + x.shape), axis, 0, 0)  28.6 us
    all_gather x1, blocking collectives, on_device(): src_block = lax.all_gather(src_embed, 'col', axis=0, tiled=True)  26.8 us
    all_gather x1, blocking collectives, on_device(): peaks_sums = lax.all_gather(jnp.stack([local_peak, local_sums]), 'col')  25.3 us
    all_gather x1, blocking collectives, on_device(): forward_all = lax.all_gather(forward_rows, 'col', axis=0, tiled=True)  17.3 us
    ppermute x4, waiting for transfers between devices, halving_sum(): got = lax.ppermute(sent, 'col', [(k, k ^ 1 << bit) for k in range(COLS)])  15.3 us
    all_to_all x2, starting transfers between devices, gather_by(): return lax.all_to_all(jnp.broadcast_to(x[None], (n,) + x.shape), axis, 0, 0)  11.8 us
    all_to_all x1, starting transfers between devices, on_device(): both = lax.all_to_all(sent, 'row', 0, 0)  10.6 us
    ppermute x4, starting transfers between devices, halving_sum(): got = lax.ppermute(sent, 'col', [(k, k ^ 1 << bit) for k in range(COLS)])  9.57 us
  transfers between devices with their start and end apart: 8, of which 6 were waited for; matrix products, arithmetic and copies ran while one was open for 4% of the time, Pallas kernels for 0%

profile of v1, /device:TPU:1, one launch (start us, length us, event | category | flops | bytes accessed | tf_op | source)
XLA Modules:
  0.0 196.5 jit_solution(4317489356233343413)
XLA Ops:
  0.6 0.0 copy-start
  0.7 1.2 copy-done
  1.9 1.1 convolution_convert_fusion.1
  3.0 0.9 broadcast_in_dim.10
  3.9 0.0 copy-start.7
  3.9 0.0 copy-start.8
  3.9 1.6 pad_maximum_fusion
  5.5 0.0 copy-start.9
  5.5 10.6 %all-to-all-start = ((bf16[32,128,256]{2,1,0:T(8,128)(2,1)}), bf16[32,128,256]{2,1,0:T(8,128)(2,1)S(1)}, u32[]{:S(2)}, u32[]{:S(2)}) async-start(bf16[32,128,256]{2,1,0:T(8,128)(2,1)} %pad_maximum_fusion), calls=%async_computation | async-start | bytes 4194304 | tf_op jit(solution)/shard_map/all_to_all | solution.py:41
  16.1 0.0 copy-done.7
  16.1 26.8 %all_gather.12 = bf16[1024,256]{1,0:T(8,128)(2,1)} all-gather(bf16[64,256]{1,0:T(8,128)(2,1)S(1)} %copy-done.7), channel_id=1, replica_groups=mesh['row'=32,'col'=16] {'col'}, dimensions={0}, use_global_device_ids=true | all-gather | bytes 557056 | tf_op jit(solution)/shard_map/all_gather | solution.py:47
  42.9 0.0 copy-done.8
  42.9 17.3 %all_gather.13 = bf16[256,1024]{1,0:T(8,128)(2,1)} all-gather(bf16[16,1024]{1,0:T(8,128)(2,1)S(1)} %copy-done.8), channel_id=1, replica_groups=mesh['row'=32,'col'=16] {'col'}, dimensions={0}, use_global_device_ids=true | all-gather | bytes 557056 | tf_op jit(solution)/shard_map/all_gather | solution.py:48
  60.2 4.4 %all-to-all-done = bf16[32,128,256]{2,1,0:T(8,128)(2,1)S(1)} async-done(((bf16[32,128,256]{2,1,0:T(8,128)(2,1)}), bf16[32,128,256]{2,1,0:T(8,128)(2,1)S(1)}, u32[]{:S(2)}, u32[]{:S(2)}) %all-to-all-start) | async-done | bytes 2097184 | tf_op jit(solution)/shard_map/all_to_all | solution.py:41
  64.6 0.2 convert_reduce_fusion.1
  64.8 0.0 copy-done.9
  64.8 1.1 broadcast_in_dim.11
  65.9 6.7 %all-to-all-start.1 = ((bf16[32,8,2048]{2,1,0:T(8,128)(2,1)}), bf16[32,8,2048]{2,1,0:T(8,128)(2,1)}, u32[]{:S(2)}, u32[]{:S(2)}) async-start(bf16[32,8,2048]{2,1,0:T(8,128)(2,1)} %broadcast_in_dim.11), calls=%async_computation.1 | async-start | bytes 2097152 | tf_op jit(solution)/shard_map/all_to_all | solution.py:15
  72.7 0.1 slice.58
  72.8 0.0 copy-start.2
  72.8 2.8 %fusion.26 = (f32[1024]{0:T(1024)S(1)}, f32[1024,2048]{1,0:T(8,128)S(1)}) fusion(bf16[1024,256]{1,0:T(8,128)(2,1)} %all_gather.12, bf16[2048,256]{1,0:T(8,128)(2,1)S(1)} %bitcast.124), kind=kOutput, calls=%fused_computation.52 | convolution fusion | flops 1075837952 | bytes 9965568 | tf_op jit(solution)/shard_map/dot_general | solution.py:52
  75.6 0.0 copy-done.2
  75.6 0.0 copy-start.1
  75.6 0.0 copy-start.6
  75.6 1.3 fusion
  76.9 1.9 copy-done.1
  78.8 25.3 %all-gather.1 = f32[16,2,1024]{2,1,0:T(2,128)S(1)} all-gather(f32[1,2,1024]{2,1,0:T(2,128)S(1)} %maximum_bitcast_fusion), channel_id=2, replica_groups=mesh['row'=32,'col'=16] {'col'}, dimensions={0}, use_global_device_ids=true | all-gather | bytes 139264 | tf_op jit(solution)/shard_map/all_gather | solution.py:58
  104.1 0.1 slice_reduce_fusion
  104.3 0.0 all-to-all-done.1
  104.3 0.0 copy-done.6
  104.3 5.3 %fusion.4 = (f32[256]{0:T(256)S(1)}, f32[256,1024]{1,0:T(8,128)S(1)}) fusion(bf16[256,1024]{1,0:T(8,128)(2,1)S(1)} %copy-done.6, f32[1024]{0:T(1024)S(1)} %get-tuple-element.8, f32[1024,2048]{1,0:T(8,128)} %copy-done.1, f32[1024]{0:T(1024)S(1)} %get-tuple-element.13, bf16[32,8,2048]{2,1,0:T(8,128)(2,1)} %all-to-all-done.1), kind=kOutput, calls=%fused_computation.14 | convolution fusion | flops 1078984448 | bytes 11019264 | tf_op jit(solution)/shard_map/dot_general | solution.py:63
  109.7 14.8 %all_to_all.33 = f32[16,1,256]{2,1,0:T(1,128)S(1)} all-to-all(f32[16,1,256]{2,1,0:T(1,128)S(1)} %broadcast_in_dim.12), channel_id=1, replica_groups=mesh['row'=32,'col'=16] {'col'}, dimensions={0} | all-to-all | bytes 32768 | tf_op jit(solution)/shard_map/all_to_all | solution.py:15
  124.5 13.8 %all_to_all.34 = f32[32,1,256]{2,1,0:T(1,128)S(1)} all-to-all(f32[32,1,256]{2,1,0:T(1,128)S(1)} %broadcast_in_dim.13), channel_id=1, replica_groups=mesh['row'=32,'col'=16] {'row'}, dimensions={0} | all-to-all | bytes 65536 | tf_op jit(solution)/shard_map/all_to_all | solution.py:15
  138.3 0.1 reduce_sum.86
  138.3 0.3 multiply_reduce_fusion
  138.6 0.7 broadcast_in_dim.14
  139.3 5.1 %all-to-all-start.4 = ((f32[16,1,1024]{2,1,0:T(1,128)}), f32[16,1,1024]{2,1,0:T(1,128)S(1)}, u32[]{:S(2)}, u32[]{:S(2)}) async-start(f32[16,1,1024]{2,1,0:T(1,128)} %broadcast_in_dim.14), calls=%async_computation.4 | async-start | bytes 131072 | tf_op jit(solution)/shard_map/all_to_all | solution.py:15
  144.4 7.8 %all-to-all-done.4 = f32[16,1,1024]{2,1,0:T(1,128)S(1)} async-done(((f32[16,1,1024]{2,1,0:T(1,128)}), f32[16,1,1024]{2,1,0:T(1,128)S(1)}, u32[]{:S(2)}, u32[]{:S(2)}) %all-to-all-start.4) | async-done | bytes 65568 | tf_op jit(solution)/shard_map/all_to_all | solution.py:15
  152.2 0.1 reduce_sum.88
  152.3 0.0 copy-start.3
  152.3 5.4 %multiply_convert_fusion = bf16[1024,2048]{1,0:T(8,128)(2,1)S(1)} fusion(f32[1024]{0:T(1024)S(1)} %reduce_sum.88, f32[1024]{0:T(1024)S(1)} %get-tuple-element.9, bf16[32,8,2048]{2,1,0:T(8,128)(2,1)} %all-to-all-done.1, bf16[256,1024]{1,0:T(8,128)(2,1)S(1)} %copy-done.6, f32[1024]{0:T(1024)S(1)} %fusion.19, f32[256]{0:T(256)S(1)} %reduce_sum.86, ...), kind=kOutput, calls=%fused_computation | convolution fusion | flops 1089732608 | bytes 14173184 | tf_op jit(solution)/shard_map/dot_general | solution.py:74
  157.6 0.0 copy-start.4
  157.6 0.0 copy-done.3
  157.7 1.3 fusion.27
  158.9 0.0 copy-start.5
  158.9 1.0 copy-done.5
  160.0 2.2 %collective-permute-start = (bf16[8,64,256]{2,1,0:T(8,128)(2,1)S(1)}, bf16[8,64,256]{2,1,0:T(8,128)(2,1)S(1)}, u32[]{:S(2)}, u32[]{:S(2)}) collective-permute-start(bf16[8,64,256]{2,1,0:T(8,128)(2,1)S(1)} %fusion.9), channel_id=1, source_target_pairs={{0,1},{1,0},{2,3},{3,2},{4,5},{5,4},{6,7},{7,6},{8,9},{9,8},{10,11... | collective-permute-start | bytes 786440 | tf_op jit(solution)/shard_map/ppermute | solution.py:26
  162.2 0.0 copy-done.4
  162.2 2.4 %convolution_convert_fusion = bf16[2048,256]{1,0:T(8,128)(2,1)} fusion(bf16[1024,2048]{1,0:T(8,128)(2,1)S(1)} %multiply_convert_fusion, bf16[1024,256]{1,0:T(8,128)(2,1)S(1)} %copy-done.4), kind=kOutput, calls=%fused_computation.4 | convolution fusion | flops 1074266112 | bytes 5767168 | tf_op jit(solution)/shard_map/dot_general | solution.py:76
  164.6 3.9 %all-to-all-start.5 = ((bf16[32,64,256]{2,1,0:T(8,128)(2,1)}), bf16[32,64,256]{2,1,0:T(8,128)(2,1)S(1)}, u32[]{:S(2)}, u32[]{:S(2)}) async-start(bf16[32,64,256]{2,1,0:T(8,128)(2,1)} %bitcast.33), calls=%async_computation.5 | async-start | bytes 2097152 | tf_op jit(solution)/shard_map/all_to_all | solution.py:77
  168.6 0.0 collective-permute-done
  168.6 1.3 fusion.8
  169.9 2.3 %collective-permute-start.1 = (bf16[4,64,256]{2,1,0:T(8,128)(2,1)S(1)}, bf16[4,64,256]{2,1,0:T(8,128)(2,1)S(1)}, u32[]{:S(2)}, u32[]{:S(2)}) collective-permute-start(bf16[4,64,256]{2,1,0:T(8,128)(2,1)S(1)} %fusion.11), channel_id=1, source_target_pairs={{0,2},{1,3},{2,0},{3,1},{4,6},{5,7},{6,4},{7,5},{8,10},{9,11},{10,... | collective-permute-start | bytes 393224 | tf_op jit(solution)/shard_map/ppermute | solution.py:26
  172.2 4.3 %collective-permute-done.1 = bf16[4,64,256]{2,1,0:T(8,128)(2,1)S(1)} collective-permute-done((bf16[4,64,256]{2,1,0:T(8,128)(2,1)S(1)}, bf16[4,64,256]{2,1,0:T(8,128)(2,1)S(1)}, u32[]{:S(2)}, u32[]{:S(2)}) %collective-permute-start.1) | collective-permute-done | bytes 131104 | tf_op jit(solution)/shard_map/ppermute | solution.py:26
  176.6 2.7 %collective-permute-start.2 = (bf16[2,64,256]{2,1,0:T(8,128)(2,1)S(1)}, bf16[2,64,256]{2,1,0:T(8,128)(2,1)S(1)}, u32[]{:S(2)}, u32[]{:S(2)}) collective-permute-start(bf16[2,64,256]{2,1,0:T(8,128)(2,1)S(1)} %fusion.17), channel_id=1, source_target_pairs={{0,4},{1,5},{2,6},{3,7},{4,0},{5,1},{6,2},{7,3},{8,12},{9,13},{10,... | collective-permute-start | bytes 196616 | tf_op jit(solution)/shard_map/ppermute | solution.py:26
  179.3 4.2 %collective-permute-done.2 = bf16[2,64,256]{2,1,0:T(8,128)(2,1)S(1)} collective-permute-done((bf16[2,64,256]{2,1,0:T(8,128)(2,1)S(1)}, bf16[2,64,256]{2,1,0:T(8,128)(2,1)S(1)}, u32[]{:S(2)}, u32[]{:S(2)}) %collective-permute-start.2) | collective-permute-done | bytes 65568 | tf_op jit(solution)/shard_map/ppermute | solution.py:26
  183.5 2.4 %collective-permute-start.3 = (bf16[1,64,256]{2,1,0:T(8,128)(2,1)S(1)}, bf16[1,64,256]{2,1,0:T(8,128)(2,1)S(1)}, u32[]{:S(2)}, u32[]{:S(2)}) collective-permute-start(bf16[1,64,256]{2,1,0:T(8,128)(2,1)S(1)} %fusion.22), channel_id=1, source_target_pairs={{0,8},{1,9},{2,10},{3,11},{4,12},{5,13},{6,14},{7,15},{8,0},{9,1},... | collective-permute-start | bytes 98312 | tf_op jit(solution)/shard_map/ppermute | solution.py:26
  185.9 6.7 %collective-permute-done.3 = bf16[1,64,256]{2,1,0:T(8,128)(2,1)S(1)} collective-permute-done((bf16[1,64,256]{2,1,0:T(8,128)(2,1)S(1)}, bf16[1,64,256]{2,1,0:T(8,128)(2,1)S(1)}, u32[]{:S(2)}, u32[]{:S(2)}) %collective-permute-start.3) | collective-permute-done | bytes 32800 | tf_op jit(solution)/shard_map/ppermute | solution.py:26
  192.7 0.6 fusion.21
  193.3 2.4 %all-to-all-done.5 = bf16[32,64,256]{2,1,0:T(8,128)(2,1)S(1)} async-done(((bf16[32,64,256]{2,1,0:T(8,128)(2,1)}), bf16[32,64,256]{2,1,0:T(8,128)(2,1)S(1)}, u32[]{:S(2)}, u32[]{:S(2)}) %all-to-all-start.5) | async-done | bytes 1048608 | tf_op jit(solution)/shard_map/all_to_all | solution.py:77
  195.8 0.8 convert_reduce_fusion
  (15 shorter events, 0.3 us)
Async XLA Ops:
  0.6 1.2 copy-start
  3.9 12.2 %copy-start.7 = (bf16[64,256]{1,0:T(8,128)(2,1)S(1)}, bf16[64,256]{1,0:T(8,128)(2,1)}, u32[]{:S(2)}) copy-start(bf16[64,256]{1,0:T(8,128)(2,1)} %param.10) | copy-start | bytes 98308
  3.9 39.0 %copy-start.8 = (bf16[16,1024]{1,0:T(8,128)(2,1)S(1)}, bf16[16,1024]{1,0:T(8,128)(2,1)}, u32[]{:S(2)}) copy-start(bf16[16,1024]{1,0:T(8,128)(2,1)} %param.8) | copy-start | bytes 98308
  5.5 59.3 %copy-start.9 = (bf16[8,2048]{1,0:T(8,128)(2,1)S(1)}, bf16[8,2048]{1,0:T(8,128)(2,1)}, u32[]{:S(2)}) copy-start(bf16[8,2048]{1,0:T(8,128)(2,1)} %param.9) | copy-start | bytes 98308
  5.5 59.1 %all-to-all-start = ((bf16[32,128,256]{2,1,0:T(8,128)(2,1)}), bf16[32,128,256]{2,1,0:T(8,128)(2,1)S(1)}, u32[]{:S(2)}, u32[]{:S(2)}) async-start(bf16[32,128,256]{2,1,0:T(8,128)(2,1)} %pad_maximum_fusion), calls=%async_computation | async-start | bytes 4194304 | tf_op jit(solution)/shard_map/all_to_all | solution.py:41
  65.9 38.4 %all-to-all-start.1 = ((bf16[32,8,2048]{2,1,0:T(8,128)(2,1)}), bf16[32,8,2048]{2,1,0:T(8,128)(2,1)}, u32[]{:S(2)}, u32[]{:S(2)}) async-start(bf16[32,8,2048]{2,1,0:T(8,128)(2,1)} %broadcast_in_dim.11), calls=%async_computation.1 | async-start | bytes 2097152 | tf_op jit(solution)/shard_map/all_to_all | solution.py:15
  72.8 2.8 %copy-start.2 = (bf16[32,64,256]{2,1,0:T(8,128)(2,1)}, bf16[32,64,256]{2,1,0:T(8,128)(2,1)S(1)}, u32[]{:S(2)}) copy-start(bf16[32,64,256]{2,1,0:T(8,128)(2,1)S(1)} %slice.58) | copy-start | bytes 3145732
  75.6 3.2 %copy-start.1 = (f32[1024,2048]{1,0:T(8,128)}, f32[1024,2048]{1,0:T(8,128)S(1)}, u32[]{:S(2)}) copy-start(f32[1024,2048]{1,0:T(8,128)S(1)} %get-tuple-element.14) | copy-start | bytes 25165828
  75.6 28.7 %copy-start.6 = (bf16[256,1024]{1,0:T(8,128)(2,1)S(1)}, bf16[256,1024]{1,0:T(8,128)(2,1)}, u32[]{:S(2)}) copy-start(bf16[256,1024]{1,0:T(8,128)(2,1)} %all_gather.13) | copy-start | bytes 1572868
  139.3 12.9 %all-to-all-start.4 = ((f32[16,1,1024]{2,1,0:T(1,128)}), f32[16,1,1024]{2,1,0:T(1,128)S(1)}, u32[]{:S(2)}, u32[]{:S(2)}) async-start(f32[16,1,1024]{2,1,0:T(1,128)} %broadcast_in_dim.14), calls=%async_computation.4 | async-start | bytes 131072 | tf_op jit(solution)/shard_map/all_to_all | solution.py:15
  152.3 5.4 %copy-start.3 = (bf16[32,64,256]{2,1,0:T(8,128)(2,1)S(1)}, bf16[32,64,256]{2,1,0:T(8,128)(2,1)}, u32[]{:S(2)}) copy-start(bf16[32,64,256]{2,1,0:T(8,128)(2,1)} %copy-done.2) | copy-start | bytes 3145732
  157.6 4.6 %copy-start.4 = (bf16[1024,256]{1,0:T(8,128)(2,1)S(1)}, bf16[1024,256]{1,0:T(8,128)(2,1)}, u32[]{:S(2)}) copy-start(bf16[1024,256]{1,0:T(8,128)(2,1)} %all_gather.12) | copy-start | bytes 1572868
  158.9 1.0 copy-start.5
  160.0 8.6 %collective-permute-start = (bf16[8,64,256]{2,1,0:T(8,128)(2,1)S(1)}, bf16[8,64,256]{2,1,0:T(8,128)(2,1)S(1)}, u32[]{:S(2)}, u32[]{:S(2)}) collective-permute-start(bf16[8,64,256]{2,1,0:T(8,128)(2,1)S(1)} %fusion.9), channel_id=1, source_target_pairs={{0,1},{1,0},{2,3},{3,2},{4,5},{5,4},{6,7},{7,6},{8,9},{9,8},{10,11... | collective-permute-start | bytes 786440 | tf_op jit(solution)/shard_map/ppermute | solution.py:26
  164.6 31.1 %all-to-all-start.5 = ((bf16[32,64,256]{2,1,0:T(8,128)(2,1)}), bf16[32,64,256]{2,1,0:T(8,128)(2,1)S(1)}, u32[]{:S(2)}, u32[]{:S(2)}) async-start(bf16[32,64,256]{2,1,0:T(8,128)(2,1)} %bitcast.33), calls=%async_computation.5 | async-start | bytes 2097152 | tf_op jit(solution)/shard_map/all_to_all | solution.py:77
  169.9 6.6 %collective-permute-start.1 = (bf16[4,64,256]{2,1,0:T(8,128)(2,1)S(1)}, bf16[4,64,256]{2,1,0:T(8,128)(2,1)S(1)}, u32[]{:S(2)}, u32[]{:S(2)}) collective-permute-start(bf16[4,64,256]{2,1,0:T(8,128)(2,1)S(1)} %fusion.11), channel_id=1, source_target_pairs={{0,2},{1,3},{2,0},{3,1},{4,6},{5,7},{6,4},{7,5},{8,10},{9,11},{10,... | collective-permute-start | bytes 393224 | tf_op jit(solution)/shard_map/ppermute | solution.py:26
  176.6 6.9 %collective-permute-start.2 = (bf16[2,64,256]{2,1,0:T(8,128)(2,1)S(1)}, bf16[2,64,256]{2,1,0:T(8,128)(2,1)S(1)}, u32[]{:S(2)}, u32[]{:S(2)}) collective-permute-start(bf16[2,64,256]{2,1,0:T(8,128)(2,1)S(1)} %fusion.17), channel_id=1, source_target_pairs={{0,4},{1,5},{2,6},{3,7},{4,0},{5,1},{6,2},{7,3},{8,12},{9,13},{10,... | collective-permute-start | bytes 196616 | tf_op jit(solution)/shard_map/ppermute | solution.py:26
  183.5 9.1 %collective-permute-start.3 = (bf16[1,64,256]{2,1,0:T(8,128)(2,1)S(1)}, bf16[1,64,256]{2,1,0:T(8,128)(2,1)S(1)}, u32[]{:S(2)}, u32[]{:S(2)}) collective-permute-start(bf16[1,64,256]{2,1,0:T(8,128)(2,1)S(1)} %fusion.22), channel_id=1, source_target_pairs={{0,8},{1,9},{2,10},{3,11},{4,12},{5,13},{6,14},{7,15},{8,0},{9,1},... | collective-permute-start | bytes 98312 | tf_op jit(solution)/shard_map/ppermute | solution.py:26

commit v2 on v1

--- a/solution.py
+++ b/solution.py
@@ -37,7 +37,7 @@
     own = SEQS // ROWS
     looked = looked.reshape(ROWS, own, -1, width).transpose(0, 2, 1, 3).reshape(ROWS, -1, width)
     depth = looked.shape[1]
-    sent = jnp.concatenate([looked, jnp.broadcast_to(tgt_embed[None], (ROWS,) + tgt_embed.shape)], axis=1)
+    sent = jnp.pad(looked, ((0, 0), (0, tgt_embed.shape[0]), (0, 0))) + jnp.pad(tgt_embed, ((depth, 0), (0, 0)))[None]
     both = lax.all_to_all(sent, "row", 0, 0)
     tgt_block = both[:, depth:].reshape(-1, width)
     own_look = jnp.sum(both[:, :depth].astype(F32), axis=0)
@@ -54,6 +54,7 @@
     exp_full = jnp.exp(logits - local_peak[:, None])
     local_sums = jnp.sum(exp_full, axis=1)
     exp_block = exp_full.astype(BF)
+    exp_block, local_sums = lax.optimization_barrier((exp_block, local_sums))
 
     peaks_sums = lax.all_gather(jnp.stack([local_peak, local_sums]), "col")
     row_peak = jnp.max(peaks_sums[:, 0], axis=0)

time: 198 us -> 194 us (0.980)
  local copies, waits for them, and re-layouts: 6.94 us -> 4.18 us
  matrix products: 18.3 us -> 15.6 us
    unnamed x20 -> x18, local copies, waits for them, and re-layouts: 4.16 us -> 1.39 us
  transfers between devices with their start and end apart: 8 -> 8, of which waited for: 6 -> 6; matrix products, arithmetic and copies ran while one was open for 4% -> 5% of each run, Pallas kernels for 0% -> 0%
where the time goes in v2:
time: 194 us; the launch traced here: 193 us
  blocking collectives  98.1 us (51%)
  starting transfers between devices  35.6 us (18%)
  waiting for transfers between devices  30.1 us (16%)
  matrix products  15.6 us (8%)
  other arithmetic  8.45 us (4%)
  local copies, waits for them, and re-layouts  4.18 us (2%)
    all_to_all x2, blocking collectives, gather_by(): return lax.all_to_all(jnp.broadcast_to(x[None], (n,) + x.shape), axis, 0, 0)  28.7 us
    all_gather x1, blocking collectives, on_device(): src_block = lax.all_gather(src_embed, 'col', axis=0, tiled=True)  26.8 us
    all_gather x1, blocking collectives, on_device(): peaks_sums = lax.all_gather(jnp.stack([local_peak, local_sums]), 'col')  25.3 us
    all_gather x1, blocking collectives, on_device(): forward_all = lax.all_gather(forward_rows, 'col', axis=0, tiled=True)  17.3 us
    ppermute x4, waiting for transfers between devices, halving_sum(): got = lax.ppermute(sent, 'col', [(k, k ^ 1 << bit) for k in range(COLS)])  15.3 us
    all_to_all x2, starting transfers between devices, gather_by(): return lax.all_to_all(jnp.broadcast_to(x[None], (n,) + x.shape), axis, 0, 0)  11.8 us
    all_to_all x1, starting transfers between devices, on_device(): both = lax.all_to_all(sent, 'row', 0, 0)  10.5 us
    ppermute x4, starting transfers between devices, halving_sum(): got = lax.ppermute(sent, 'col', [(k, k ^ 1 << bit) for k in range(COLS)])  9.33 us
  transfers between devices with their start and end apart: 8, of which 6 were waited for; matrix products, arithmetic and copies ran while one was open for 5% of the time, Pallas kernels for 0%

profile of v2, /device:TPU:1, one launch (start us, length us, event | category | flops | bytes accessed | tf_op | source)
XLA Modules:
  0.0 192.9 jit_solution(8056559997596078077)
XLA Ops:
  0.6 0.0 copy-start
  0.7 0.8 pad.9
  1.5 0.4 copy-done
  1.9 1.1 convolution_convert_fusion.1
  3.0 0.0 copy-start.6
  3.0 0.0 copy-start.7
  3.1 0.0 copy-start.8
  3.1 1.7 pad_add_fusion
  4.8 10.5 %all-to-all-start = ((bf16[32,128,256]{2,1,0:T(8,128)(2,1)}), bf16[32,128,256]{2,1,0:T(8,128)(2,1)S(1)}, u32[]{:S(2)}, u32[]{:S(2)}) async-start(bf16[32,128,256]{2,1,0:T(8,128)(2,1)} %pad_add_fusion), calls=%async_computation | async-start | bytes 4194304 | tf_op jit(solution)/shard_map/all_to_all | solution.py:41
  15.3 0.0 copy-done.6
  15.3 26.8 %all_gather.12 = bf16[1024,256]{1,0:T(8,128)(2,1)} all-gather(bf16[64,256]{1,0:T(8,128)(2,1)S(1)} %copy-done.6), channel_id=1, replica_groups=mesh['row'=32,'col'=16] {'col'}, dimensions={0}, use_global_device_ids=true | all-gather | bytes 557056 | tf_op jit(solution)/shard_map/all_gather | solution.py:47
  42.1 0.0 copy-done.7
  42.1 17.3 %all_gather.13 = bf16[256,1024]{1,0:T(8,128)(2,1)} all-gather(bf16[16,1024]{1,0:T(8,128)(2,1)S(1)} %copy-done.7), channel_id=1, replica_groups=mesh['row'=32,'col'=16] {'col'}, dimensions={0}, use_global_device_ids=true | all-gather | bytes 557056 | tf_op jit(solution)/shard_map/all_gather | solution.py:48
  59.4 4.4 %all-to-all-done = bf16[32,128,256]{2,1,0:T(8,128)(2,1)S(1)} async-done(((bf16[32,128,256]{2,1,0:T(8,128)(2,1)}), bf16[32,128,256]{2,1,0:T(8,128)(2,1)S(1)}, u32[]{:S(2)}, u32[]{:S(2)}) %all-to-all-start) | async-done | bytes 2097184 | tf_op jit(solution)/shard_map/all_to_all | solution.py:41
  63.8 0.2 convert_reduce_fusion.1
  64.0 0.0 copy-done.8
  64.0 1.1 broadcast_in_dim.8
  65.1 6.7 %all-to-all-start.1 = ((bf16[32,8,2048]{2,1,0:T(8,128)(2,1)}), bf16[32,8,2048]{2,1,0:T(8,128)(2,1)}, u32[]{:S(2)}, u32[]{:S(2)}) async-start(bf16[32,8,2048]{2,1,0:T(8,128)(2,1)} %broadcast_in_dim.8), calls=%async_computation.1 | async-start | bytes 2097152 | tf_op jit(solution)/shard_map/all_to_all | solution.py:15
  71.9 0.1 slice.58
  72.0 0.0 copy-start.1
  72.0 2.8 %fusion.25 = (f32[1024]{0:T(1024)S(1)}, f32[1024,2048]{1,0:T(8,128)S(1)}) fusion(bf16[1024,256]{1,0:T(8,128)(2,1)} %all_gather.12, bf16[2048,256]{1,0:T(8,128)(2,1)S(1)} %bitcast.125), kind=kOutput, calls=%fused_computation.52 | convolution fusion | flops 1075837952 | bytes 9965568 | tf_op jit(solution)/shard_map/dot_general | solution.py:52
  74.8 0.0 copy-done.1
  74.8 0.0 copy-start.5
  74.8 3.0 %fusion = (f32[1024]{0:T(1024)S(1)}, bf16[1024,2048]{1,0:T(8,128)(2,1)}) fusion(f32[1024,2048]{1,0:T(8,128)S(1)} %get-tuple-element.20, f32[1024]{0:T(1024)S(1)} %get-tuple-element.19), kind=kLoop, calls=%fused_computation.2 | loop fusion | flops 6290432 | bytes 12591104 | tf_op jit(solution)/shard_map/reduce_sum | solution.py:55
  77.8 25.3 %all-gather.1 = f32[16,2,1024]{2,1,0:T(2,128)S(1)} all-gather(f32[1,2,1024]{2,1,0:T(2,128)S(1)} %maximum_bitcast_fusion), channel_id=2, replica_groups=mesh['row'=32,'col'=16] {'col'}, dimensions={0}, use_global_device_ids=true | all-gather | bytes 139264 | tf_op jit(solution)/shard_map/all_gather | solution.py:59
  103.1 0.1 slice_reduce_fusion
  103.3 0.0 all-to-all-done.1
  103.3 0.0 copy-done.5
  103.3 3.9 %fusion.4 = (f32[256]{0:T(256)S(1)}, f32[256,1024]{1,0:T(8,128)S(1)}) fusion(bf16[256,1024]{1,0:T(8,128)(2,1)S(1)} %copy-done.5, f32[1024]{0:T(1024)S(1)} %get-tuple-element.12, bf16[1024,2048]{1,0:T(8,128)(2,1)} %get-tuple-element.8, bf16[32,8,2048]{2,1,0:T(8,128)(2,1)} %all-to-all-done.1), kind=kOutput, calls=%fused_computation.14 | convolution fusion | flops 1074790144 | bytes 6820864 | tf_op jit(solution)/shard_map/dot_general | solution.py:64
  107.3 14.9 %all_to_all.33 = f32[16,1,256]{2,1,0:T(1,128)S(1)} all-to-all(f32[16,1,256]{2,1,0:T(1,128)S(1)} %broadcast_in_dim.9), channel_id=1, replica_groups=mesh['row'=32,'col'=16] {'col'}, dimensions={0} | all-to-all | bytes 32768 | tf_op jit(solution)/shard_map/all_to_all | solution.py:15
  122.3 13.8 %all_to_all.34 = f32[32,1,256]{2,1,0:T(1,128)S(1)} all-to-all(f32[32,1,256]{2,1,0:T(1,128)S(1)} %broadcast_in_dim.10), channel_id=1, replica_groups=mesh['row'=32,'col'=16] {'row'}, dimensions={0} | all-to-all | bytes 65536 | tf_op jit(solution)/shard_map/all_to_all | solution.py:15
  136.1 0.1 reduce_sum.86
  136.1 0.3 multiply_reduce_fusion
  136.4 0.7 broadcast_in_dim.11
  137.1 5.1 %all-to-all-start.4 = ((f32[16,1,1024]{2,1,0:T(1,128)}), f32[16,1,1024]{2,1,0:T(1,128)S(1)}, u32[]{:S(2)}, u32[]{:S(2)}) async-start(f32[16,1,1024]{2,1,0:T(1,128)} %broadcast_in_dim.11), calls=%async_computation.4 | async-start | bytes 131072 | tf_op jit(solution)/shard_map/all_to_all | solution.py:15
  142.2 7.8 %all-to-all-done.4 = f32[16,1,1024]{2,1,0:T(1,128)S(1)} async-done(((f32[16,1,1024]{2,1,0:T(1,128)}), f32[16,1,1024]{2,1,0:T(1,128)S(1)}, u32[]{:S(2)}, u32[]{:S(2)}) %all-to-all-start.4) | async-done | bytes 65568 | tf_op jit(solution)/shard_map/all_to_all | solution.py:15
  150.0 0.1 reduce_sum.88
  150.1 0.0 copy-start.2
  150.1 4.1 %multiply_convert_fusion = bf16[1024,2048]{1,0:T(8,128)(2,1)S(1)} fusion(bf16[1024,2048]{1,0:T(8,128)(2,1)} %get-tuple-element.8, f32[1024]{0:T(1024)S(1)} %reduce_sum.88, f32[1024]{0:T(1024)S(1)} %get-tuple-element.13, bf16[32,8,2048]{2,1,0:T(8,128)(2,1)} %all-to-all-done.1, bf16[256,1024]{1,0:T(8,128)(2,1)S(1)} %copy-done.5, f32[1024]{0:T(1024)S(1)} %fusion.19, ...), kind=kOutput, calls=%fused_computation | convolution fusion | flops 1085538304 | bytes 9974784 | tf_op jit(solution)/shard_map/dot_general | solution.py:75
  154.1 0.0 copy-start.3
  154.2 0.0 copy-done.2
  154.2 1.3 fusion.26
  155.4 0.0 copy-start.4
  155.4 1.0 copy-done.4
  156.5 2.1 %collective-permute-start = (bf16[8,64,256]{2,1,0:T(8,128)(2,1)S(1)}, bf16[8,64,256]{2,1,0:T(8,128)(2,1)S(1)}, u32[]{:S(2)}, u32[]{:S(2)}) collective-permute-start(bf16[8,64,256]{2,1,0:T(8,128)(2,1)S(1)} %fusion.9), channel_id=1, source_target_pairs={{0,1},{1,0},{2,3},{3,2},{4,5},{5,4},{6,7},{7,6},{8,9},{9,8},{10,11... | collective-permute-start | bytes 786440 | tf_op jit(solution)/shard_map/ppermute | solution.py:26
  158.5 0.0 copy-done.3
  158.5 2.4 %convolution_convert_fusion = bf16[2048,256]{1,0:T(8,128)(2,1)} fusion(bf16[1024,2048]{1,0:T(8,128)(2,1)S(1)} %multiply_convert_fusion, bf16[1024,256]{1,0:T(8,128)(2,1)S(1)} %copy-done.3), kind=kOutput, calls=%fused_computation.4 | convolution fusion | flops 1074266112 | bytes 5767168 | tf_op jit(solution)/shard_map/dot_general | solution.py:77
  161.0 3.9 %all-to-all-start.5 = ((bf16[32,64,256]{2,1,0:T(8,128)(2,1)}), bf16[32,64,256]{2,1,0:T(8,128)(2,1)S(1)}, u32[]{:S(2)}, u32[]{:S(2)}) async-start(bf16[32,64,256]{2,1,0:T(8,128)(2,1)} %bitcast.33), calls=%async_computation.5 | async-start | bytes 2097152 | tf_op jit(solution)/shard_map/all_to_all | solution.py:78
  164.9 0.0 collective-permute-done
  164.9 1.3 fusion.8
  166.3 2.3 %collective-permute-start.1 = (bf16[4,64,256]{2,1,0:T(8,128)(2,1)S(1)}, bf16[4,64,256]{2,1,0:T(8,128)(2,1)S(1)}, u32[]{:S(2)}, u32[]{:S(2)}) collective-permute-start(bf16[4,64,256]{2,1,0:T(8,128)(2,1)S(1)} %fusion.11), channel_id=1, source_target_pairs={{0,2},{1,3},{2,0},{3,1},{4,6},{5,7},{6,4},{7,5},{8,10},{9,11},{10,... | collective-permute-start | bytes 393224 | tf_op jit(solution)/shard_map/ppermute | solution.py:26
  168.6 4.3 %collective-permute-done.1 = bf16[4,64,256]{2,1,0:T(8,128)(2,1)S(1)} collective-permute-done((bf16[4,64,256]{2,1,0:T(8,128)(2,1)S(1)}, bf16[4,64,256]{2,1,0:T(8,128)(2,1)S(1)}, u32[]{:S(2)}, u32[]{:S(2)}) %collective-permute-start.1) | collective-permute-done | bytes 131104 | tf_op jit(solution)/shard_map/ppermute | solution.py:26
  173.0 2.6 %collective-permute-start.2 = (bf16[2,64,256]{2,1,0:T(8,128)(2,1)S(1)}, bf16[2,64,256]{2,1,0:T(8,128)(2,1)S(1)}, u32[]{:S(2)}, u32[]{:S(2)}) collective-permute-start(bf16[2,64,256]{2,1,0:T(8,128)(2,1)S(1)} %fusion.17), channel_id=1, source_target_pairs={{0,4},{1,5},{2,6},{3,7},{4,0},{5,1},{6,2},{7,3},{8,12},{9,13},{10,... | collective-permute-start | bytes 196616 | tf_op jit(solution)/shard_map/ppermute | solution.py:26
  175.6 4.3 %collective-permute-done.2 = bf16[2,64,256]{2,1,0:T(8,128)(2,1)S(1)} collective-permute-done((bf16[2,64,256]{2,1,0:T(8,128)(2,1)S(1)}, bf16[2,64,256]{2,1,0:T(8,128)(2,1)S(1)}, u32[]{:S(2)}, u32[]{:S(2)}) %collective-permute-start.2) | collective-permute-done | bytes 65568 | tf_op jit(solution)/shard_map/ppermute | solution.py:26
  179.9 2.4 %collective-permute-start.3 = (bf16[1,64,256]{2,1,0:T(8,128)(2,1)S(1)}, bf16[1,64,256]{2,1,0:T(8,128)(2,1)S(1)}, u32[]{:S(2)}, u32[]{:S(2)}) collective-permute-start(bf16[1,64,256]{2,1,0:T(8,128)(2,1)S(1)} %fusion.22), channel_id=1, source_target_pairs={{0,8},{1,9},{2,10},{3,11},{4,12},{5,13},{6,14},{7,15},{8,0},{9,1},... | collective-permute-start | bytes 98312 | tf_op jit(solution)/shard_map/ppermute | solution.py:26
  182.3 6.7 %collective-permute-done.3 = bf16[1,64,256]{2,1,0:T(8,128)(2,1)S(1)} collective-permute-done((bf16[1,64,256]{2,1,0:T(8,128)(2,1)S(1)}, bf16[1,64,256]{2,1,0:T(8,128)(2,1)S(1)}, u32[]{:S(2)}, u32[]{:S(2)}) %collective-permute-start.3) | collective-permute-done | bytes 32800 | tf_op jit(solution)/shard_map/ppermute | solution.py:26
  189.0 0.6 fusion.21
  189.7 2.5 %all-to-all-done.5 = bf16[32,64,256]{2,1,0:T(8,128)(2,1)S(1)} async-done(((bf16[32,64,256]{2,1,0:T(8,128)(2,1)}), bf16[32,64,256]{2,1,0:T(8,128)(2,1)S(1)}, u32[]{:S(2)}, u32[]{:S(2)}) %all-to-all-start.5) | async-done | bytes 1048608 | tf_op jit(solution)/shard_map/all_to_all | solution.py:78
  192.2 0.8 convert_reduce_fusion
  (15 shorter events, 0.3 us)
Async XLA Ops:
  0.6 1.2 copy-start
  3.0 12.3 %copy-start.6 = (bf16[64,256]{1,0:T(8,128)(2,1)S(1)}, bf16[64,256]{1,0:T(8,128)(2,1)}, u32[]{:S(2)}) copy-start(bf16[64,256]{1,0:T(8,128)(2,1)} %param.10) | copy-start | bytes 98308
  3.0 39.1 %copy-start.7 = (bf16[16,1024]{1,0:T(8,128)(2,1)S(1)}, bf16[16,1024]{1,0:T(8,128)(2,1)}, u32[]{:S(2)}) copy-start(bf16[16,1024]{1,0:T(8,128)(2,1)} %param.8) | copy-start | bytes 98308
  3.1 60.9 %copy-start.8 = (bf16[8,2048]{1,0:T(8,128)(2,1)S(1)}, bf16[8,2048]{1,0:T(8,128)(2,1)}, u32[]{:S(2)}) copy-start(bf16[8,2048]{1,0:T(8,128)(2,1)} %param.9) | copy-start | bytes 98308
  4.8 59.0 %all-to-all-start = ((bf16[32,128,256]{2,1,0:T(8,128)(2,1)}), bf16[32,128,256]{2,1,0:T(8,128)(2,1)S(1)}, u32[]{:S(2)}, u32[]{:S(2)}) async-start(bf16[32,128,256]{2,1,0:T(8,128)(2,1)} %pad_add_fusion), calls=%async_computation | async-start | bytes 4194304 | tf_op jit(solution)/shard_map/all_to_all | solution.py:41
  65.1 38.2 %all-to-all-start.1 = ((bf16[32,8,2048]{2,1,0:T(8,128)(2,1)}), bf16[32,8,2048]{2,1,0:T(8,128)(2,1)}, u32[]{:S(2)}, u32[]{:S(2)}) async-start(bf16[32,8,2048]{2,1,0:T(8,128)(2,1)} %broadcast_in_dim.8), calls=%async_computation.1 | async-start | bytes 2097152 | tf_op jit(solution)/shard_map/all_to_all | solution.py:15
  72.0 2.8 %copy-start.1 = (bf16[32,64,256]{2,1,0:T(8,128)(2,1)}, bf16[32,64,256]{2,1,0:T(8,128)(2,1)S(1)}, u32[]{:S(2)}) copy-start(bf16[32,64,256]{2,1,0:T(8,128)(2,1)S(1)} %slice.58) | copy-start | bytes 3145732
  74.8 28.6 %copy-start.5 = (bf16[256,1024]{1,0:T(8,128)(2,1)S(1)}, bf16[256,1024]{1,0:T(8,128)(2,1)}, u32[]{:S(2)}) copy-start(bf16[256,1024]{1,0:T(8,128)(2,1)} %all_gather.13) | copy-start | bytes 1572868
  137.1 12.9 %all-to-all-start.4 = ((f32[16,1,1024]{2,1,0:T(1,128)}), f32[16,1,1024]{2,1,0:T(1,128)S(1)}, u32[]{:S(2)}, u32[]{:S(2)}) async-start(f32[16,1,1024]{2,1,0:T(1,128)} %broadcast_in_dim.11), calls=%async_computation.4 | async-start | bytes 131072 | tf_op jit(solution)/shard_map/all_to_all | solution.py:15
  150.1 4.1 %copy-start.2 = (bf16[32,64,256]{2,1,0:T(8,128)(2,1)S(1)}, bf16[32,64,256]{2,1,0:T(8,128)(2,1)}, u32[]{:S(2)}) copy-start(bf16[32,64,256]{2,1,0:T(8,128)(2,1)} %copy-done.1) | copy-start | bytes 3145732
  154.1 4.4 %copy-start.3 = (bf16[1024,256]{1,0:T(8,128)(2,1)S(1)}, bf16[1024,256]{1,0:T(8,128)(2,1)}, u32[]{:S(2)}) copy-start(bf16[1024,256]{1,0:T(8,128)(2,1)} %all_gather.12) | copy-start | bytes 1572868
  155.4 1.0 copy-start.4
  156.5 8.4 %collective-permute-start = (bf16[8,64,256]{2,1,0:T(8,128)(2,1)S(1)}, bf16[8,64,256]{2,1,0:T(8,128)(2,1)S(1)}, u32[]{:S(2)}, u32[]{:S(2)}) collective-permute-start(bf16[8,64,256]{2,1,0:T(8,128)(2,1)S(1)} %fusion.9), channel_id=1, source_target_pairs={{0,1},{1,0},{2,3},{3,2},{4,5},{5,4},{6,7},{7,6},{8,9},{9,8},{10,11... | collective-permute-start | bytes 786440 | tf_op jit(solution)/shard_map/ppermute | solution.py:26
  161.0 31.2 %all-to-all-start.5 = ((bf16[32,64,256]{2,1,0:T(8,128)(2,1)}), bf16[32,64,256]{2,1,0:T(8,128)(2,1)S(1)}, u32[]{:S(2)}, u32[]{:S(2)}) async-start(bf16[32,64,256]{2,1,0:T(8,128)(2,1)} %bitcast.33), calls=%async_computation.5 | async-start | bytes 2097152 | tf_op jit(solution)/shard_map/all_to_all | solution.py:78
  166.3 6.6 %collective-permute-start.1 = (bf16[4,64,256]{2,1,0:T(8,128)(2,1)S(1)}, bf16[4,64,256]{2,1,0:T(8,128)(2,1)S(1)}, u32[]{:S(2)}, u32[]{:S(2)}) collective-permute-start(bf16[4,64,256]{2,1,0:T(8,128)(2,1)S(1)} %fusion.11), channel_id=1, source_target_pairs={{0,2},{1,3},{2,0},{3,1},{4,6},{5,7},{6,4},{7,5},{8,10},{9,11},{10,... | collective-permute-start | bytes 393224 | tf_op jit(solution)/shard_map/ppermute | solution.py:26
  173.0 6.9 %collective-permute-start.2 = (bf16[2,64,256]{2,1,0:T(8,128)(2,1)S(1)}, bf16[2,64,256]{2,1,0:T(8,128)(2,1)S(1)}, u32[]{:S(2)}, u32[]{:S(2)}) collective-permute-start(bf16[2,64,256]{2,1,0:T(8,128)(2,1)S(1)} %fusion.17), channel_id=1, source_target_pairs={{0,4},{1,5},{2,6},{3,7},{4,0},{5,1},{6,2},{7,3},{8,12},{9,13},{10,... | collective-permute-start | bytes 196616 | tf_op jit(solution)/shard_map/ppermute | solution.py:26
  179.9 9.1 %collective-permute-start.3 = (bf16[1,64,256]{2,1,0:T(8,128)(2,1)S(1)}, bf16[1,64,256]{2,1,0:T(8,128)(2,1)S(1)}, u32[]{:S(2)}, u32[]{:S(2)}) collective-permute-start(bf16[1,64,256]{2,1,0:T(8,128)(2,1)S(1)} %fusion.22), channel_id=1, source_target_pairs={{0,8},{1,9},{2,10},{3,11},{4,12},{5,13},{6,14},{7,15},{8,0},{9,1},... | collective-permute-start | bytes 98312 | tf_op jit(solution)/shard_map/ppermute | solution.py:26

commit v3 on v2

--- a/solution.py
+++ b/solution.py
@@ -15,17 +15,20 @@
     return lax.all_to_all(jnp.broadcast_to(x[None], (n,) + x.shape), axis, 0, 0)
 
 
-def halving_sum(parts):
+def column_sum(kept, sent):
     me = lax.axis_index("col")
-    held = parts
-    for bit in range(4):
-        pairs = held.reshape((held.shape[0] // 2, 2) + held.shape[1:])
-        mine = (me >> bit) & 1
-        kept = jnp.where(mine == 0, pairs[:, 0], pairs[:, 1])
-        sent = jnp.where(mine == 0, pairs[:, 1], pairs[:, 0]).astype(BF)
-        got = lax.ppermute(sent, "col", [(k, k ^ (1 << bit)) for k in range(COLS)])
-        held = kept + got.astype(F32)
-    return held[0]
+    held = kept + lax.ppermute(sent, "col", [(k, k ^ 1) for k in range(COLS)]).astype(F32)
+    fours = held.reshape((4, -1) + held.shape[1:])
+    mine = me >> 2
+    total = lax.dynamic_index_in_dim(fours, mine, 0, keepdims=False)
+    for d in (1, 2, 3):
+        sent = lax.dynamic_index_in_dim(fours, mine ^ d, 0, keepdims=False).astype(BF)
+        total = total + lax.ppermute(sent, "col", [(k, k ^ (4 * d)) for k in range(COLS)]).astype(F32)
+    mine = (me >> 1) & 1
+    last = 2
+    kept = jnp.where(mine == 0, total[0], total[1])
+    sent = jnp.where(mine == 0, total[1], total[0]).astype(BF)
+    return kept + lax.ppermute(sent, "col", [(k, k ^ last) for k in range(COLS)]).astype(F32)
 
 
 def on_device(tokens, emission_table, forward_rows, backward_rows, src_embed, tgt_embed):
@@ -74,10 +77,15 @@
 
     summed = lax.dot_general(coeffs, weighted, (((0,), (0,)), ((), ())), preferred_element_type=F32)
     grad_logits = (exp_block.astype(F32) * scale[:, None] * (summed - ratio[:, None])).astype(BF)
+    src_part = jnp.dot(grad_logits, tgt_block, preferred_element_type=F32)
+    pairs = src_part.reshape((COLS // 2, 2) + src_embed.shape)
+    mine = lax.axis_index("col") & 1
+    kept = jnp.where(mine == 0, pairs[:, 0], pairs[:, 1])
+    sent = jnp.where(mine == 0, pairs[:, 1], pairs[:, 0]).astype(BF)
+    kept, sent, grad_logits = lax.optimization_barrier((kept, sent, grad_logits))
+    grad_src = column_sum(kept, sent)
     tgt_part = lax.dot_general(grad_logits, src_block, (((0,), (0,)), ((), ())), preferred_element_type=F32)
     tgt_parts = lax.all_to_all(tgt_part.astype(BF).reshape((ROWS,) + tgt_embed.shape), "row", 0, 0)
-    src_part = jnp.dot(grad_logits, tgt_block, preferred_element_type=F32)
-    grad_src = halving_sum(src_part.reshape((COLS,) + src_embed.shape))
     grad_tgt = jnp.sum(tgt_parts.astype(F32), axis=0)
     return (grad_src, grad_tgt)
 

time: 194 us -> 191 us (0.985)
  waiting for transfers between devices: 30.1 us -> 20.8 us
  starting transfers between devices: 35.6 us -> 44.8 us
    ppermute x4 -> x5, waiting for transfers between devices: 15.3 us -> 5.73 us  [the longest x3 2.8 us: column_sum(): lax.ppermute(sent, 'col', [(k, k ^ 4 * d) for k in range(COLS)]).astype(F32)]
    ppermute x4 -> x5, starting transfers between devices: 9.33 us -> 18.5 us  [the longest x3 11.4 us: column_sum(): lax.ppermute(sent, 'col', [(k, k ^ 4 * d) for k in range(COLS)]).astype(F32)]
  transfers between devices with their start and end apart: 8 -> 9, of which waited for: 6 -> 7; matrix products, arithmetic and copies ran while one was open for 5% -> 4% of each run, Pallas kernels for 0% -> 0%
where the time goes in v3:
time: 191 us
  blocking collectives  98.1 us (51%)
  starting transfers between devices  44.8 us (23%)
  waiting for transfers between devices  20.8 us (11%)
  matrix products  15.5 us (8%)
  other arithmetic  7.19 us (4%)
  local copies, waits for them, and re-layouts  3.23 us (2%)
    all_to_all x2, blocking collectives, gather_by(): return lax.all_to_all(jnp.broadcast_to(x[None], (n,) + x.shape), axis, 0, 0)  28.7 us
    all_gather x1, blocking collectives, on_device(): src_block = lax.all_gather(src_embed, 'col', axis=0, tiled=True)  26.8 us
    all_gather x1, blocking collectives, on_device(): peaks_sums = lax.all_gather(jnp.stack([local_peak, local_sums]), 'col')  25.3 us
    all_gather x1, blocking collectives, on_device(): forward_all = lax.all_gather(forward_rows, 'col', axis=0, tiled=True)  17.3 us
    all_to_all x2, starting transfers between devices, gather_by(): return lax.all_to_all(jnp.broadcast_to(x[None], (n,) + x.shape), axis, 0, 0)  11.8 us
    ppermute x3, starting transfers between devices, column_sum(): lax.ppermute(sent, 'col', [(k, k ^ 4 * d) for k in range(COLS)]).astype(F32)  11.4 us
    all_to_all x1, starting transfers between devices, on_device(): both = lax.all_to_all(sent, 'row', 0, 0)  10.5 us
    all_to_all x2, waiting for transfers between devices, gather_by(): return lax.all_to_all(jnp.broadcast_to(x[None], (n,) + x.shape), axis, 0, 0)  7.84 us
  transfers between devices with their start and end apart: 9, of which 7 were waited for; matrix products, arithmetic and copies ran while one was open for 4% of the time, Pallas kernels for 0%

profile of v3, /device:TPU:1, one launch (start us, length us, event | category | flops | bytes accessed | tf_op | source)
XLA Modules:
  0.0 190.7 jit_solution(10188660506502464241)
XLA Ops:
  0.6 0.0 copy-start
  0.7 0.8 pad.9
  1.5 0.4 copy-done
  1.9 1.1 convolution_convert_fusion.1
  3.0 0.0 copy-start.5
  3.0 0.0 copy-start.6
  3.1 0.0 copy-start.7
  3.1 1.7 pad_add_fusion
  4.8 10.5 %all-to-all-start = ((bf16[32,128,256]{2,1,0:T(8,128)(2,1)}), bf16[32,128,256]{2,1,0:T(8,128)(2,1)S(1)}, u32[]{:S(2)}, u32[]{:S(2)}) async-start(bf16[32,128,256]{2,1,0:T(8,128)(2,1)} %pad_add_fusion), calls=%async_computation | async-start | bytes 4194304 | tf_op jit(solution)/shard_map/all_to_all | solution.py:44
  15.3 0.0 copy-done.5
  15.3 26.8 %all_gather.12 = bf16[1024,256]{1,0:T(8,128)(2,1)} all-gather(bf16[64,256]{1,0:T(8,128)(2,1)S(1)} %copy-done.5), channel_id=1, replica_groups=mesh['row'=32,'col'=16] {'col'}, dimensions={0}, use_global_device_ids=true | all-gather | bytes 557056 | tf_op jit(solution)/shard_map/all_gather | solution.py:50
  42.1 0.0 copy-done.6
  42.1 17.3 %all_gather.13 = bf16[256,1024]{1,0:T(8,128)(2,1)} all-gather(bf16[16,1024]{1,0:T(8,128)(2,1)S(1)} %copy-done.6), channel_id=1, replica_groups=mesh['row'=32,'col'=16] {'col'}, dimensions={0}, use_global_device_ids=true | all-gather | bytes 557056 | tf_op jit(solution)/shard_map/all_gather | solution.py:51
  59.4 4.4 %all-to-all-done = bf16[32,128,256]{2,1,0:T(8,128)(2,1)S(1)} async-done(((bf16[32,128,256]{2,1,0:T(8,128)(2,1)}), bf16[32,128,256]{2,1,0:T(8,128)(2,1)S(1)}, u32[]{:S(2)}, u32[]{:S(2)}) %all-to-all-start) | async-done | bytes 2097184 | tf_op jit(solution)/shard_map/all_to_all | solution.py:44
  63.8 0.2 convert_reduce_fusion.1
  64.0 0.0 copy-done.7
  64.0 1.1 broadcast_in_dim.8
  65.1 6.7 %all-to-all-start.1 = ((bf16[32,8,2048]{2,1,0:T(8,128)(2,1)}), bf16[32,8,2048]{2,1,0:T(8,128)(2,1)}, u32[]{:S(2)}, u32[]{:S(2)}) async-start(bf16[32,8,2048]{2,1,0:T(8,128)(2,1)} %broadcast_in_dim.8), calls=%async_computation.1 | async-start | bytes 2097152 | tf_op jit(solution)/shard_map/all_to_all | solution.py:15
  71.9 0.1 slice.38
  72.0 0.0 copy-start.1
  72.0 2.8 %fusion.23 = (f32[1024]{0:T(1024)S(1)}, f32[1024,2048]{1,0:T(8,128)S(1)}) fusion(bf16[1024,256]{1,0:T(8,128)(2,1)} %all_gather.12, bf16[2048,256]{1,0:T(8,128)(2,1)S(1)} %bitcast.82), kind=kOutput, calls=%fused_computation.49 | convolution fusion | flops 1075837952 | bytes 9965568 | tf_op jit(solution)/shard_map/dot_general | solution.py:55
  74.8 0.0 copy-done.1
  74.8 0.0 copy-start.4
  74.8 3.0 %fusion = (f32[1024]{0:T(1024)S(1)}, bf16[1024,2048]{1,0:T(8,128)(2,1)}) fusion(f32[1024,2048]{1,0:T(8,128)S(1)} %get-tuple-element.29, f32[1024]{0:T(1024)S(1)} %get-tuple-element.28), kind=kLoop, calls=%fused_computation.2 | loop fusion | flops 6290432 | bytes 12591104 | tf_op jit(solution)/shard_map/reduce_sum | solution.py:58
  77.8 25.3 %all-gather.1 = f32[16,2,1024]{2,1,0:T(2,128)S(1)} all-gather(f32[1,2,1024]{2,1,0:T(2,128)S(1)} %maximum_bitcast_fusion), channel_id=2, replica_groups=mesh['row'=32,'col'=16] {'col'}, dimensions={0}, use_global_device_ids=true | all-gather | bytes 139264 | tf_op jit(solution)/shard_map/all_gather | solution.py:62
  103.1 0.1 slice_reduce_fusion
  103.3 0.0 all-to-all-done.1
  103.3 0.0 copy-done.4
  103.3 3.9 %fusion.4 = (f32[256]{0:T(256)S(1)}, f32[256,1024]{1,0:T(8,128)S(1)}) fusion(bf16[256,1024]{1,0:T(8,128)(2,1)S(1)} %copy-done.4, f32[1024]{0:T(1024)S(1)} %get-tuple-element.18, bf16[1024,2048]{1,0:T(8,128)(2,1)} %get-tuple-element.11, bf16[32,8,2048]{2,1,0:T(8,128)(2,1)} %all-to-all-done.1), kind=kOutput, calls=%fused_computation.14 | convolution fusion | flops 1074790144 | bytes 6820864 | tf_op jit(solution)/shard_map/dot_general | solution.py:67
  107.3 14.9 %all_to_all.33 = f32[16,1,256]{2,1,0:T(1,128)S(1)} all-to-all(f32[16,1,256]{2,1,0:T(1,128)S(1)} %broadcast_in_dim.9), channel_id=1, replica_groups=mesh['row'=32,'col'=16] {'col'}, dimensions={0} | all-to-all | bytes 32768 | tf_op jit(solution)/shard_map/all_to_all | solution.py:15
  122.3 13.8 %all_to_all.34 = f32[32,1,256]{2,1,0:T(1,128)S(1)} all-to-all(f32[32,1,256]{2,1,0:T(1,128)S(1)} %broadcast_in_dim.10), channel_id=1, replica_groups=mesh['row'=32,'col'=16] {'row'}, dimensions={0} | all-to-all | bytes 65536 | tf_op jit(solution)/shard_map/all_to_all | solution.py:15
  136.1 0.1 reduce_sum.86
  136.1 0.3 multiply_reduce_fusion
  136.4 0.7 broadcast_in_dim.11
  137.1 5.1 %all-to-all-start.4 = ((f32[16,1,1024]{2,1,0:T(1,128)}), f32[16,1,1024]{2,1,0:T(1,128)S(1)}, u32[]{:S(2)}, u32[]{:S(2)}) async-start(f32[16,1,1024]{2,1,0:T(1,128)} %broadcast_in_dim.11), calls=%async_computation.4 | async-start | bytes 131072 | tf_op jit(solution)/shard_map/all_to_all | solution.py:15
  142.2 7.8 %all-to-all-done.4 = f32[16,1,1024]{2,1,0:T(1,128)S(1)} async-done(((f32[16,1,1024]{2,1,0:T(1,128)}), f32[16,1,1024]{2,1,0:T(1,128)S(1)}, u32[]{:S(2)}, u32[]{:S(2)}) %all-to-all-start.4) | async-done | bytes 65568 | tf_op jit(solution)/shard_map/all_to_all | solution.py:15
  150.0 0.1 reduce_sum.88
  150.1 0.0 copy-start.2
  150.1 4.1 %multiply_convert_fusion = bf16[1024,2048]{1,0:T(8,128)(2,1)S(1)} fusion(bf16[1024,2048]{1,0:T(8,128)(2,1)} %get-tuple-element.11, f32[1024]{0:T(1024)S(1)} %reduce_sum.88, f32[1024]{0:T(1024)S(1)} %get-tuple-element.19, bf16[32,8,2048]{2,1,0:T(8,128)(2,1)} %all-to-all-done.1, bf16[256,1024]{1,0:T(8,128)(2,1)S(1)} %copy-done.4, f32[1024]{0:T(1024)S(1)} %fusion.18, ...), kind=kOutput, calls=%fused_computation | convolution fusion | flops 1085538304 | bytes 9974784 | tf_op jit(solution)/shard_map/dot_general | solution.py:78
  154.1 0.0 copy-done.2
  154.2 0.0 copy-start.3
  154.2 1.3 fusion.24
  155.4 0.1 fusion.7
  155.5 0.1 fusion.8
  155.6 0.0 copy-done.3
  155.6 2.4 %convolution_convert_fusion = bf16[2048,256]{1,0:T(8,128)(2,1)} fusion(bf16[1024,2048]{1,0:T(8,128)(2,1)S(1)} %multiply_convert_fusion, bf16[1024,256]{1,0:T(8,128)(2,1)S(1)} %copy-done.3), kind=kOutput, calls=%fused_computation.4 | convolution fusion | flops 1074266112 | bytes 5767168 | tf_op jit(solution)/shard_map/dot_general | solution.py:87
  158.0 3.9 %all-to-all-start.5 = ((bf16[32,64,256]{2,1,0:T(8,128)(2,1)}), bf16[32,64,256]{2,1,0:T(8,128)(2,1)S(1)}, u32[]{:S(2)}, u32[]{:S(2)}) async-start(bf16[32,64,256]{2,1,0:T(8,128)(2,1)} %bitcast.86), calls=%async_computation.5 | async-start | bytes 2097152 | tf_op jit(solution)/shard_map/all_to_all | solution.py:88
  161.9 2.1 %collective-permute-start = (bf16[8,64,256]{2,1,0:T(8,128)(2,1)S(1)}, bf16[8,64,256]{2,1,0:T(8,128)(2,1)S(1)}, u32[]{:S(2)}, u32[]{:S(2)}) collective-permute-start(bf16[8,64,256]{2,1,0:T(8,128)(2,1)S(1)} %fusion.8), channel_id=1, source_target_pairs={{0,1},{1,0},{2,3},{3,2},{4,5},{5,4},{6,7},{7,6},{8,9},{9,8},{10,11... | collective-permute-start | bytes 786440 | tf_op jit(solution)/shard_map/ppermute | solution.py:20
  164.0 1.3 collective-permute-done
  165.3 0.1 convert_add_fusion
  165.4 2.2 %collective-permute-start.1 = (bf16[2,64,256]{2,1,0:T(8,128)(2,1)S(1)}, bf16[2,64,256]{2,1,0:T(8,128)(2,1)S(1)}, u32[]{:S(2)}, u32[]{:S(2)}) collective-permute-start(bf16[2,64,256]{2,1,0:T(8,128)(2,1)S(1)} %get-tuple-element.22), channel_id=1, source_target_pairs={{0,4},{1,5},{2,6},{3,7},{4,0},{5,1},{6,2},{7,3},{8,12},{9,13},{10,... | collective-permute-start | bytes 196616 | tf_op jit(solution)/shard_map/ppermute | solution.py:26
  167.6 4.0 %collective-permute-start.2 = (bf16[2,64,256]{2,1,0:T(8,128)(2,1)S(1)}, bf16[2,64,256]{2,1,0:T(8,128)(2,1)S(1)}, u32[]{:S(2)}, u32[]{:S(2)}) collective-permute-start(bf16[2,64,256]{2,1,0:T(8,128)(2,1)S(1)} %get-tuple-element.24), channel_id=1, source_target_pairs={{0,8},{1,9},{2,10},{3,11},{4,12},{5,13},{6,14},{7,15},{8,0},{9,1},... | collective-permute-start | bytes 196616 | tf_op jit(solution)/shard_map/ppermute | solution.py:26
  171.6 5.2 %collective-permute-start.3 = (bf16[2,64,256]{2,1,0:T(8,128)(2,1)S(1)}, bf16[2,64,256]{2,1,0:T(8,128)(2,1)S(1)}, u32[]{:S(2)}, u32[]{:S(2)}) collective-permute-start(bf16[2,64,256]{2,1,0:T(8,128)(2,1)S(1)} %get-tuple-element.23), channel_id=1, source_target_pairs={{0,12},{1,13},{2,14},{3,15},{4,8},{5,9},{6,10},{7,11},{8,4},{9,5},... | collective-permute-start | bytes 196616 | tf_op jit(solution)/shard_map/ppermute | solution.py:26
  176.8 0.0 collective-permute-done.1
  176.8 1.5 collective-permute-done.2
  178.3 1.3 collective-permute-done.3
  179.7 5.1 %collective-permute-start.4 = (bf16[64,256]{1,0:T(8,128)(2,1)S(1)}, bf16[64,256]{1,0:T(8,128)(2,1)S(1)}, u32[]{:S(2)}, u32[]{:S(2)}) collective-permute-start(bf16[64,256]{1,0:T(8,128)(2,1)S(1)} %fusion.20), channel_id=1, source_target_pairs={{0,2},{1,3},{2,0},{3,1},{4,6},{5,7},{6,4},{7,5},{8,10},{9,11},{10,... | collective-permute-start | bytes 98312 | tf_op jit(solution)/shard_map/ppermute | solution.py:31
  184.8 1.6 collective-permute-done.4
  186.4 0.6 bitcast_add_fusion.1
  187.0 2.8 %all-to-all-done.5 = bf16[32,64,256]{2,1,0:T(8,128)(2,1)S(1)} async-done(((bf16[32,64,256]{2,1,0:T(8,128)(2,1)}), bf16[32,64,256]{2,1,0:T(8,128)(2,1)S(1)}, u32[]{:S(2)}, u32[]{:S(2)}) %all-to-all-start.5) | async-done | bytes 1048608 | tf_op jit(solution)/shard_map/all_to_all | solution.py:88
  189.9 0.8 convert_reduce_fusion
  (12 shorter events, 0.2 us)
Async XLA Ops:
  0.6 1.2 copy-start
  3.0 12.3 %copy-start.5 = (bf16[64,256]{1,0:T(8,128)(2,1)S(1)}, bf16[64,256]{1,0:T(8,128)(2,1)}, u32[]{:S(2)}) copy-start(bf16[64,256]{1,0:T(8,128)(2,1)} %param.10) | copy-start | bytes 98308
  3.0 39.1 %copy-start.6 = (bf16[16,1024]{1,0:T(8,128)(2,1)S(1)}, bf16[16,1024]{1,0:T(8,128)(2,1)}, u32[]{:S(2)}) copy-start(bf16[16,1024]{1,0:T(8,128)(2,1)} %param.8) | copy-start | bytes 98308
  3.1 60.9 %copy-start.7 = (bf16[8,2048]{1,0:T(8,128)(2,1)S(1)}, bf16[8,2048]{1,0:T(8,128)(2,1)}, u32[]{:S(2)}) copy-start(bf16[8,2048]{1,0:T(8,128)(2,1)} %param.9) | copy-start | bytes 98308
  4.8 59.0 %all-to-all-start = ((bf16[32,128,256]{2,1,0:T(8,128)(2,1)}), bf16[32,128,256]{2,1,0:T(8,128)(2,1)S(1)}, u32[]{:S(2)}, u32[]{:S(2)}) async-start(bf16[32,128,256]{2,1,0:T(8,128)(2,1)} %pad_add_fusion), calls=%async_computation | async-start | bytes 4194304 | tf_op jit(solution)/shard_map/all_to_all | solution.py:44
  65.1 38.2 %all-to-all-start.1 = ((bf16[32,8,2048]{2,1,0:T(8,128)(2,1)}), bf16[32,8,2048]{2,1,0:T(8,128)(2,1)}, u32[]{:S(2)}, u32[]{:S(2)}) async-start(bf16[32,8,2048]{2,1,0:T(8,128)(2,1)} %broadcast_in_dim.8), calls=%async_computation.1 | async-start | bytes 2097152 | tf_op jit(solution)/shard_map/all_to_all | solution.py:15
  72.0 2.8 %copy-start.1 = (bf16[32,64,256]{2,1,0:T(8,128)(2,1)}, bf16[32,64,256]{2,1,0:T(8,128)(2,1)S(1)}, u32[]{:S(2)}) copy-start(bf16[32,64,256]{2,1,0:T(8,128)(2,1)S(1)} %slice.38) | copy-start | bytes 3145732
  74.8 28.6 %copy-start.4 = (bf16[256,1024]{1,0:T(8,128)(2,1)S(1)}, bf16[256,1024]{1,0:T(8,128)(2,1)}, u32[]{:S(2)}) copy-start(bf16[256,1024]{1,0:T(8,128)(2,1)} %all_gather.13) | copy-start | bytes 1572868
  137.1 12.9 %all-to-all-start.4 = ((f32[16,1,1024]{2,1,0:T(1,128)}), f32[16,1,1024]{2,1,0:T(1,128)S(1)}, u32[]{:S(2)}, u32[]{:S(2)}) async-start(f32[16,1,1024]{2,1,0:T(1,128)} %broadcast_in_dim.11), calls=%async_computation.4 | async-start | bytes 131072 | tf_op jit(solution)/shard_map/all_to_all | solution.py:15
  150.1 4.1 %copy-start.2 = (bf16[32,64,256]{2,1,0:T(8,128)(2,1)S(1)}, bf16[32,64,256]{2,1,0:T(8,128)(2,1)}, u32[]{:S(2)}) copy-start(bf16[32,64,256]{2,1,0:T(8,128)(2,1)} %copy-done.1) | copy-start | bytes 3145732
  154.2 1.4 copy-start.3
  158.0 31.9 %all-to-all-start.5 = ((bf16[32,64,256]{2,1,0:T(8,128)(2,1)}), bf16[32,64,256]{2,1,0:T(8,128)(2,1)S(1)}, u32[]{:S(2)}, u32[]{:S(2)}) async-start(bf16[32,64,256]{2,1,0:T(8,128)(2,1)} %bitcast.86), calls=%async_computation.5 | async-start | bytes 2097152 | tf_op jit(solution)/shard_map/all_to_all | solution.py:88
  161.9 3.4 %collective-permute-start = (bf16[8,64,256]{2,1,0:T(8,128)(2,1)S(1)}, bf16[8,64,256]{2,1,0:T(8,128)(2,1)S(1)}, u32[]{:S(2)}, u32[]{:S(2)}) collective-permute-start(bf16[8,64,256]{2,1,0:T(8,128)(2,1)S(1)} %fusion.8), channel_id=1, source_target_pairs={{0,1},{1,0},{2,3},{3,2},{4,5},{5,4},{6,7},{7,6},{8,9},{9,8},{10,11... | collective-permute-start | bytes 786440 | tf_op jit(solution)/shard_map/ppermute | solution.py:20
  165.4 11.4 %collective-permute-start.1 = (bf16[2,64,256]{2,1,0:T(8,128)(2,1)S(1)}, bf16[2,64,256]{2,1,0:T(8,128)(2,1)S(1)}, u32[]{:S(2)}, u32[]{:S(2)}) collective-permute-start(bf16[2,64,256]{2,1,0:T(8,128)(2,1)S(1)} %get-tuple-element.22), channel_id=1, source_target_pairs={{0,4},{1,5},{2,6},{3,7},{4,0},{5,1},{6,2},{7,3},{8,12},{9,13},{10,... | collective-permute-start | bytes 196616 | tf_op jit(solution)/shard_map/ppermute | solution.py:26
  167.6 10.7 %collective-permute-start.2 = (bf16[2,64,256]{2,1,0:T(8,128)(2,1)S(1)}, bf16[2,64,256]{2,1,0:T(8,128)(2,1)S(1)}, u32[]{:S(2)}, u32[]{:S(2)}) collective-permute-start(bf16[2,64,256]{2,1,0:T(8,128)(2,1)S(1)} %get-tuple-element.24), channel_id=1, source_target_pairs={{0,8},{1,9},{2,10},{3,11},{4,12},{5,13},{6,14},{7,15},{8,0},{9,1},... | collective-permute-start | bytes 196616 | tf_op jit(solution)/shard_map/ppermute | solution.py:26
  171.6 8.0 %collective-permute-start.3 = (bf16[2,64,256]{2,1,0:T(8,128)(2,1)S(1)}, bf16[2,64,256]{2,1,0:T(8,128)(2,1)S(1)}, u32[]{:S(2)}, u32[]{:S(2)}) collective-permute-start(bf16[2,64,256]{2,1,0:T(8,128)(2,1)S(1)} %get-tuple-element.23), channel_id=1, source_target_pairs={{0,12},{1,13},{2,14},{3,15},{4,8},{5,9},{6,10},{7,11},{8,4},{9,5},... | collective-permute-start | bytes 196616 | tf_op jit(solution)/shard_map/ppermute | solution.py:26
  179.7 6.7 %collective-permute-start.4 = (bf16[64,256]{1,0:T(8,128)(2,1)S(1)}, bf16[64,256]{1,0:T(8,128)(2,1)S(1)}, u32[]{:S(2)}, u32[]{:S(2)}) collective-permute-start(bf16[64,256]{1,0:T(8,128)(2,1)S(1)} %fusion.20), channel_id=1, source_target_pairs={{0,2},{1,3},{2,0},{3,1},{4,6},{5,7},{6,4},{7,5},{8,10},{9,11},{10,... | collective-permute-start | bytes 98312 | tf_op jit(solution)/shard_map/ppermute | solution.py:31

commit v4 on v3

--- a/solution.py
+++ b/solution.py
@@ -7,6 +7,9 @@
 SEQS = 256
 ROWS = 32
 COLS = 16
+XS = 4
+YS = 8
+ALONG_Y = [[y * XS + x for y in range(YS)] for x in range(XS)]
 BF = jnp.bfloat16
 F32 = jnp.float32
 
@@ -31,6 +34,22 @@
     return kept + lax.ppermute(sent, "col", [(k, k ^ last) for k in range(COLS)]).astype(F32)
 
 
+def thirds(x):
+    high = lax.reduce_precision(x, 8, 7)
+    middle = lax.reduce_precision(x - high, 8, 7)
+    return jnp.concatenate([high, middle, x - high - middle], axis=0).astype(BF)
+
+
+def in_order(parts):
+    x = lax.axis_index("row") % XS
+    a, b, c, d = parts
+    low = x & 1
+    a, b, c, d = (jnp.where(low == 0, p, q) for p, q in ((a, b), (b, a), (c, d), (d, c)))
+    high = x >> 1
+    a, b, c, d = (jnp.where(high == 0, p, q) for p, q in ((a, c), (b, d), (c, a), (d, b)))
+    return jnp.stack([a, b, c, d], axis=1)
+
+
 def on_device(tokens, emission_table, forward_rows, backward_rows, src_embed, tgt_embed):
     vocab_local = emission_table.shape[0]
     offset = lax.axis_index("row") * vocab_local
@@ -38,18 +57,18 @@
     looked = jnp.dot(onehot, emission_table, preferred_element_type=F32).astype(BF)
     width = tgt_embed.shape[1]
     own = SEQS // ROWS
-    looked = looked.reshape(ROWS, own, -1, width).transpose(0, 2, 1, 3).reshape(ROWS, -1, width)
-    depth = looked.shape[1]
-    sent = jnp.pad(looked, ((0, 0), (0, tgt_embed.shape[0]), (0, 0))) + jnp.pad(tgt_embed, ((depth, 0), (0, 0)))[None]
-    both = lax.all_to_all(sent, "row", 0, 0)
-    tgt_block = both[:, depth:].reshape(-1, width)
-    own_look = jnp.sum(both[:, :depth].astype(F32), axis=0)
-    own_look = own_look.reshape(-1, own, width).transpose(1, 0, 2).reshape(own, -1)
+    looks = lax.all_to_all(looked.reshape(ROWS, own, -1), "row", 0, 0)
+    own_look = jnp.sum(looks.astype(F32), axis=0)
     own_weighted = (jnp.exp(own_look) * backward_rows.astype(F32)).astype(BF)
 
+    held = lax.all_to_all(
+        jnp.broadcast_to(tgt_embed[None], (YS,) + tgt_embed.shape), "row", 0, 0, axis_index_groups=ALONG_Y
+    )
+    others = [lax.ppermute(held, "row", [(k, k ^ d) for k in range(ROWS)]) for d in (1, 2, 3)]
     src_block = lax.all_gather(src_embed, "col", axis=0, tiled=True)
-    forward_all = lax.all_gather(forward_rows, "col", axis=0, tiled=True)
-    own_weighted, src_block, forward_all = lax.optimization_barrier((own_weighted, src_block, forward_all))
+    *others, src_block = lax.optimization_barrier((*others, src_block))
+    tgt_block = in_order([held] + others).reshape(-1, width)
+    tgt_block, own_weighted = lax.optimization_barrier((tgt_block, own_weighted))
     weighted = gather_by(own_weighted, "row", ROWS).reshape(SEQS, -1)
 
     logits = lax.dot_general(src_block, tgt_block, (((1,), (1,)), ((), ())), preferred_element_type=F32)
@@ -59,7 +78,11 @@
     exp_block = exp_full.astype(BF)
     exp_block, local_sums = lax.optimization_barrier((exp_block, local_sums))
 
-    peaks_sums = lax.all_gather(jnp.stack([local_peak, local_sums]), "col")
+    local = thirds(jnp.stack([local_peak, local_sums]))
+    got = lax.all_gather(jnp.concatenate([forward_rows, local], axis=0), "col")
+    forward_all = lax.optimization_barrier(got[:, : forward_rows.shape[0]].reshape(SEQS, -1))
+    peaks_sums = got[:, forward_rows.shape[0] :].astype(F32)
+    peaks_sums = (peaks_sums[:, :2] + peaks_sums[:, 2:4]) + peaks_sums[:, 4:]
     row_peak = jnp.max(peaks_sums[:, 0], axis=0)
     row_sums = jnp.sum(peaks_sums[:, 1] * jnp.exp(peaks_sums[:, 0] - row_peak[None]), axis=0)
     scale = jnp.exp(local_peak - row_peak)

time: 191 us -> 189 us (0.990)
  blocking collectives: 98.1 us -> 70.7 us
  starting transfers between devices: 44.8 us -> 60.7 us
  waiting for transfers between devices: 20.8 us -> 27.9 us
    all_gather x2 -> x1, blocking collectives: 42.6 us -> 16.9 us  [on_device(): got = lax.all_gather(jnp.concatenate([forward_rows, local], axis=0), 'col')]
    ppermute x0 -> x3, starting transfers between devices: none -> 9.58 us  [on_device(): lax.ppermute(held, 'row', [(k, k ^ d) for k in range(ROWS)])]
    all_to_all x2, waiting for transfers between devices: 7.84 us -> 12.1 us  [gather_by(): return lax.all_to_all(jnp.broadcast_to(x[None], (n,) + x.shape), axis, 0, 0)]
    all_to_all x1 -> x2, starting transfers between devices: 10.5 us -> 14.2 us  [the longest x1 7.65 us: on_device(): lax.all_to_all(jnp.broadcast_to(tgt_embed[None], (YS,) + tgt_embed.shape)...]
    all_to_all x2, blocking collectives: 28.7 us -> 25.6 us  [gather_by(): return lax.all_to_all(jnp.broadcast_to(x[None], (n,) + x.shape), axis, 0, 0)]
    all_to_all x1 -> x2, waiting for transfers between devices: 4.4 us -> 7.25 us  [the longest x1 7.25 us: on_device(): lax.all_to_all(jnp.broadcast_to(tgt_embed[None], (YS,) + tgt_embed.shape)...]
    all_to_all x2, starting transfers between devices: 11.8 us -> 14.4 us  [gather_by(): return lax.all_to_all(jnp.broadcast_to(x[None], (n,) + x.shape), axis, 0, 0)]
  transfers between devices with their start and end apart: 9 -> 13, of which waited for: 7 -> 8; matrix products, arithmetic and copies ran while one was open for 4% -> 5% of each run, Pallas kernels for 0% -> 0%
where the time goes in v4:
time: 189 us; the launch traced here: 188 us
  blocking collectives  70.7 us (37%)
  starting transfers between devices  60.7 us (32%)
  waiting for transfers between devices  27.9 us (15%)
  matrix products  17 us (9%)
  other arithmetic  7.1 us (4%)
  local copies, waits for them, and re-layouts  3.51 us (2%)
    all_gather x1, blocking collectives, on_device(): src_block = lax.all_gather(src_embed, 'col', axis=0, tiled=True)  28.2 us
    all_to_all x2, blocking collectives, gather_by(): return lax.all_to_all(jnp.broadcast_to(x[None], (n,) + x.shape), axis, 0, 0)  25.6 us
    all_gather x1, blocking collectives, on_device(): got = lax.all_gather(jnp.concatenate([forward_rows, local], axis=0), 'col')  16.9 us
    all_to_all x2, starting transfers between devices, gather_by(): return lax.all_to_all(jnp.broadcast_to(x[None], (n,) + x.shape), axis, 0, 0)  14.4 us
    all_to_all x2, waiting for transfers between devices, gather_by(): return lax.all_to_all(jnp.broadcast_to(x[None], (n,) + x.shape), axis, 0, 0)  12.1 us
    ppermute x3, starting transfers between devices, column_sum(): lax.ppermute(sent, 'col', [(k, k ^ 4 * d) for k in range(COLS)]).astype(F32)  11.4 us
    ppermute x3, starting transfers between devices, on_device(): lax.ppermute(held, 'row', [(k, k ^ d) for k in range(ROWS)])  9.58 us
    all_to_all x1, starting transfers between devices, on_device(): lax.all_to_all(jnp.broadcast_to(tgt_embed[None], (YS,) + tgt_embed.shape)...  7.65 us
  transfers between devices with their start and end apart: 13, of which 8 were waited for; matrix products, arithmetic and copies ran while one was open for 5% of the time, Pallas kernels for 0%

profile of v4, /device:TPU:1, one launch (start us, length us, event | category | flops | bytes accessed | tf_op | source)
XLA Modules:
  0.0 187.9 jit_solution(1997467472189663879)
XLA Ops:
  0.6 0.0 copy-start
  0.6 0.0 copy-start.2
  0.7 1.6 broadcast_in_dim.10
  2.2 7.7 %all-to-all-start = ((bf16[8,64,256]{2,1,0:T(8,128)(2,1)}), bf16[8,64,256]{2,1,0:T(8,128)(2,1)S(1)}, u32[]{:S(2)}, u32[]{:S(2)}) async-start(bf16[8,64,256]{2,1,0:T(8,128)(2,1)} %broadcast_in_dim.10), calls=%async_computation | async-start | bytes 524288 | tf_op jit(solution)/shard_map/all_to_all | solution.py:64
  9.9 0.0 copy-done
  9.9 2.1 %fusion.2 = bf16[32,8,2048]{2,1,0:T(8,128)(2,1)} fusion(bf16[256,2048]{1,0:T(8,128)(2,1)S(1)} %copy-done, s32[256]{0:T(256)S(1)} %iota_add_fusion, s32[256]{0:T(256)} %param.6), kind=kOutput, calls=%fused_computation.6 | convolution fusion | flops 269025280 | bytes 2099200 | tf_op jit(solution)/shard_map/dot_general | solution.py:57
  12.0 0.0 copy-start.4
  12.1 7.2 %all-to-all-done = bf16[8,64,256]{2,1,0:T(8,128)(2,1)S(1)} async-done(((bf16[8,64,256]{2,1,0:T(8,128)(2,1)}), bf16[8,64,256]{2,1,0:T(8,128)(2,1)S(1)}, u32[]{:S(2)}, u32[]{:S(2)}) %all-to-all-start) | async-done | bytes 262176 | tf_op jit(solution)/shard_map/all_to_all | solution.py:64
  19.3 6.6 %all-to-all-start.1 = ((bf16[32,8,2048]{2,1,0:T(8,128)(2,1)}), bf16[32,8,2048]{2,1,0:T(8,128)(2,1)S(1)}, u32[]{:S(2)}, u32[]{:S(2)}) async-start(bf16[32,8,2048]{2,1,0:T(8,128)(2,1)} %fusion.2), calls=%async_computation.1 | async-start | bytes 2097152 | tf_op jit(solution)/shard_map/all_to_all | solution.py:60
  25.9 3.1 %collective-permute-start = (bf16[8,64,256]{2,1,0:T(8,128)(2,1)S(1)}, bf16[8,64,256]{2,1,0:T(8,128)(2,1)S(1)}, u32[]{:S(2)}, u32[]{:S(2)}) collective-permute-start(bf16[8,64,256]{2,1,0:T(8,128)(2,1)S(1)} %all-to-all-done), channel_id=1, source_target_pairs={{0,16},{16,0},{32,48},{48,32},{64,80},{80,64},{96,112},{112,96},{1... | collective-permute-start | bytes 786440 | tf_op jit(solution)/shard_map/ppermute | solution.py:67
  29.0 4.3 %collective-permute-start.1 = (bf16[8,64,256]{2,1,0:T(8,128)(2,1)S(1)}, bf16[8,64,256]{2,1,0:T(8,128)(2,1)S(1)}, u32[]{:S(2)}, u32[]{:S(2)}) collective-permute-start(bf16[8,64,256]{2,1,0:T(8,128)(2,1)S(1)} %all-to-all-done), channel_id=1, source_target_pairs={{0,32},{16,48},{32,0},{48,16},{64,96},{80,112},{96,64},{112,80},{1... | collective-permute-start | bytes 786440 | tf_op jit(solution)/shard_map/ppermute | solution.py:67
  33.3 2.1 %collective-permute-start.2 = (bf16[8,64,256]{2,1,0:T(8,128)(2,1)S(1)}, bf16[8,64,256]{2,1,0:T(8,128)(2,1)S(1)}, u32[]{:S(2)}, u32[]{:S(2)}) collective-permute-start(bf16[8,64,256]{2,1,0:T(8,128)(2,1)S(1)} %all-to-all-done), channel_id=1, source_target_pairs={{0,48},{16,32},{32,16},{48,0},{64,112},{80,96},{96,80},{112,64},{1... | collective-permute-start | bytes 786440 | tf_op jit(solution)/shard_map/ppermute | solution.py:67
  35.5 0.0 copy-done.2
  35.5 28.2 %all_gather.9 = bf16[1024,256]{1,0:T(8,128)(2,1)} all-gather(bf16[64,256]{1,0:T(8,128)(2,1)S(1)} %copy-done.2), channel_id=1, replica_groups=mesh['row'=32,'col'=16] {'col'}, dimensions={0}, use_global_device_ids=true | all-gather | bytes 557056 | tf_op jit(solution)/shard_map/all_gather | solution.py:68
  63.7 0.0 collective-permute-done
  63.7 0.0 collective-permute-done.1
  63.7 0.0 collective-permute-done.2
  63.7 0.1 select_bitcast_fusion.3
  63.8 0.1 pad_maximum_fusion
  64.0 0.0 all-to-all-done.1
  64.0 0.2 convert_reduce_fusion.1
  64.1 0.0 copy-done.4
  64.2 1.1 broadcast_in_dim.11
  65.3 9.3 %all-to-all-start.2 = ((bf16[32,8,2048]{2,1,0:T(8,128)(2,1)}), bf16[32,8,2048]{2,1,0:T(8,128)(2,1)}, u32[]{:S(2)}, u32[]{:S(2)}) async-start(bf16[32,8,2048]{2,1,0:T(8,128)(2,1)} %broadcast_in_dim.11), calls=%async_computation.2 | async-start | bytes 2097152 | tf_op jit(solution)/shard_map/all_to_all | solution.py:18
  74.7 2.4 %fusion.26 = (f32[1024]{0:T(1024)S(1)}, f32[1024,2048]{1,0:T(8,128)S(1)}) fusion(bf16[1024,256]{1,0:T(8,128)(2,1)} %all_gather.9, bf16[2048,256]{1,0:T(8,128)(2,1)S(1)} %bitcast.84), kind=kOutput, calls=%fused_computation.67 | convolution fusion | flops 1075837952 | bytes 9965568 | tf_op jit(solution)/shard_map/dot_general | solution.py:74
  77.1 0.0 copy-start.3
  77.1 3.0 %fusion = (f32[1024]{0:T(1024)S(1)}, bf16[1024,2048]{1,0:T(8,128)(2,1)}) fusion(f32[1024,2048]{1,0:T(8,128)S(1)} %get-tuple-element.42, f32[1024]{0:T(1024)S(1)} %get-tuple-element.41), kind=kLoop, calls=%fused_computation.2 | loop fusion | flops 6290432 | bytes 12591104 | tf_op jit(solution)/shard_map/reduce_sum | solution.py:77
  80.1 0.0 copy-done.3
  80.2 16.9 %all-gather.1 = bf16[16,22,1024]{2,1,0:T(8,128)(2,1)S(1)} all-gather(bf16[1,22,1024]{2,1,0:T(8,128)(2,1)S(1)} %maximum_bitcast_fusion), channel_id=2, replica_groups=mesh['row'=32,'col'=16] {'col'}, dimensions={0}, use_global_device_ids=true | all-gather | bytes 765952 | tf_op jit(solution)/shard_map/all_gather | solution.py:82
  97.2 0.1 slice_add_fusion
  97.3 0.1 slice_reduce_fusion
  97.5 4.2 %all-to-all-done.2 = bf16[32,8,2048]{2,1,0:T(8,128)(2,1)} async-done(((bf16[32,8,2048]{2,1,0:T(8,128)(2,1)}), bf16[32,8,2048]{2,1,0:T(8,128)(2,1)}, u32[]{:S(2)}, u32[]{:S(2)}) %all-to-all-start.2) | async-done | bytes 1048608 | tf_op jit(solution)/shard_map/all_to_all | solution.py:18
  101.7 4.8 %fusion.5 = (f32[256]{0:T(256)S(1)}, f32[256,1024]{1,0:T(8,128)}) fusion(bf16[256,1024]{1,0:T(8,128)(2,1)S(1)} %bitcast.88, f32[1024]{0:T(1024)S(1)} %get-tuple-element.24, bf16[1024,2048]{1,0:T(8,128)(2,1)} %get-tuple-element.18, bf16[32,8,2048]{2,1,0:T(8,128)(2,1)} %all-to-all-done.2), kind=kOutput, calls=%fused_computation.14 | convolution fusion | flops 1074790144 | bytes 6820864 | tf_op jit(solution)/shard_map/dot_general | solution.py:90
  106.6 11.8 %all_to_all.38 = f32[16,1,256]{2,1,0:T(1,128)S(1)} all-to-all(f32[16,1,256]{2,1,0:T(1,128)S(1)} %broadcast_in_dim.12), channel_id=1, replica_groups=mesh['row'=32,'col'=16] {'col'}, dimensions={0} | all-to-all | bytes 32768 | tf_op jit(solution)/shard_map/all_to_all | solution.py:18
  118.4 13.8 %all_to_all.39 = f32[32,1,256]{2,1,0:T(1,128)S(1)} all-to-all(f32[32,1,256]{2,1,0:T(1,128)S(1)} %broadcast_in_dim.13), channel_id=1, replica_groups=mesh['row'=32,'col'=16] {'row'}, dimensions={0} | all-to-all | bytes 65536 | tf_op jit(solution)/shard_map/all_to_all | solution.py:18
  132.2 0.1 reduce_sum.86
  132.2 1.5 multiply_reduce_fusion
  133.8 0.7 broadcast_in_dim.14
  134.4 5.1 %all-to-all-start.5 = ((f32[16,1,1024]{2,1,0:T(1,128)}), f32[16,1,1024]{2,1,0:T(1,128)S(1)}, u32[]{:S(2)}, u32[]{:S(2)}) async-start(f32[16,1,1024]{2,1,0:T(1,128)} %broadcast_in_dim.14), calls=%async_computation.5 | async-start | bytes 131072 | tf_op jit(solution)/shard_map/all_to_all | solution.py:18
  139.5 7.8 %all-to-all-done.5 = f32[16,1,1024]{2,1,0:T(1,128)S(1)} async-done(((f32[16,1,1024]{2,1,0:T(1,128)}), f32[16,1,1024]{2,1,0:T(1,128)S(1)}, u32[]{:S(2)}, u32[]{:S(2)}) %all-to-all-start.5) | async-done | bytes 65568 | tf_op jit(solution)/shard_map/all_to_all | solution.py:18
  147.3 0.1 reduce_sum.88
  147.4 4.0 %multiply_convert_fusion = bf16[1024,2048]{1,0:T(8,128)(2,1)S(1)} fusion(bf16[1024,2048]{1,0:T(8,128)(2,1)} %get-tuple-element.18, f32[1024]{0:T(1024)S(1)} %reduce_sum.88, f32[1024]{0:T(1024)S(1)} %get-tuple-element.25, bf16[32,8,2048]{2,1,0:T(8,128)(2,1)} %all-to-all-done.2, bf16[256,1024]{1,0:T(8,128)(2,1)S(1)} %bitcast.90, f32[1024]{0:T(1024)S(1)} %fusion.21, ...), kind=kOutput, calls=%fused_computation | convolution fusion | flops 1085538304 | bytes 9974784 | tf_op jit(solution)/shard_map/dot_general | solution.py:101
  151.4 0.0 copy-start.1
  151.4 1.3 fusion.27
  152.7 0.1 fusion.8
  152.8 0.1 fusion.9
  152.8 0.0 copy-done.1
  152.8 2.4 %convolution_convert_fusion = bf16[2048,256]{1,0:T(8,128)(2,1)} fusion(bf16[1024,2048]{1,0:T(8,128)(2,1)S(1)} %multiply_convert_fusion, bf16[1024,256]{1,0:T(8,128)(2,1)S(1)} %copy-done.1), kind=kOutput, calls=%fused_computation.4 | convolution fusion | flops 1074266112 | bytes 5767168 | tf_op jit(solution)/shard_map/dot_general | solution.py:110
  155.2 3.9 %all-to-all-start.6 = ((bf16[32,64,256]{2,1,0:T(8,128)(2,1)}), bf16[32,64,256]{2,1,0:T(8,128)(2,1)S(1)}, u32[]{:S(2)}, u32[]{:S(2)}) async-start(bf16[32,64,256]{2,1,0:T(8,128)(2,1)} %bitcast.93), calls=%async_computation.6 | async-start | bytes 2097152 | tf_op jit(solution)/shard_map/all_to_all | solution.py:111
  159.1 2.1 %collective-permute-start.3 = (bf16[8,64,256]{2,1,0:T(8,128)(2,1)S(1)}, bf16[8,64,256]{2,1,0:T(8,128)(2,1)S(1)}, u32[]{:S(2)}, u32[]{:S(2)}) collective-permute-start(bf16[8,64,256]{2,1,0:T(8,128)(2,1)S(1)} %fusion.9), channel_id=1, source_target_pairs={{0,1},{1,0},{2,3},{3,2},{4,5},{5,4},{6,7},{7,6},{8,9},{9,8},{10,11... | collective-permute-start | bytes 786440 | tf_op jit(solution)/shard_map/ppermute | solution.py:23
  161.2 1.3 collective-permute-done.3
  162.6 0.1 convert_add_fusion
  162.7 2.2 %collective-permute-start.4 = (bf16[2,64,256]{2,1,0:T(8,128)(2,1)S(1)}, bf16[2,64,256]{2,1,0:T(8,128)(2,1)S(1)}, u32[]{:S(2)}, u32[]{:S(2)}) collective-permute-start(bf16[2,64,256]{2,1,0:T(8,128)(2,1)S(1)} %get-tuple-element.32), channel_id=1, source_target_pairs={{0,4},{1,5},{2,6},{3,7},{4,0},{5,1},{6,2},{7,3},{8,12},{9,13},{10,... | collective-permute-start | bytes 196616 | tf_op jit(solution)/shard_map/ppermute | solution.py:29
  164.9 4.0 %collective-permute-start.5 = (bf16[2,64,256]{2,1,0:T(8,128)(2,1)S(1)}, bf16[2,64,256]{2,1,0:T(8,128)(2,1)S(1)}, u32[]{:S(2)}, u32[]{:S(2)}) collective-permute-start(bf16[2,64,256]{2,1,0:T(8,128)(2,1)S(1)} %get-tuple-element.34), channel_id=1, source_target_pairs={{0,8},{1,9},{2,10},{3,11},{4,12},{5,13},{6,14},{7,15},{8,0},{9,1},... | collective-permute-start | bytes 196616 | tf_op jit(solution)/shard_map/ppermute | solution.py:29
  168.9 5.2 %collective-permute-start.6 = (bf16[2,64,256]{2,1,0:T(8,128)(2,1)S(1)}, bf16[2,64,256]{2,1,0:T(8,128)(2,1)S(1)}, u32[]{:S(2)}, u32[]{:S(2)}) collective-permute-start(bf16[2,64,256]{2,1,0:T(8,128)(2,1)S(1)} %get-tuple-element.33), channel_id=1, source_target_pairs={{0,12},{1,13},{2,14},{3,15},{4,8},{5,9},{6,10},{7,11},{8,4},{9,5},... | collective-permute-start | bytes 196616 | tf_op jit(solution)/shard_map/ppermute | solution.py:29
  174.1 0.0 collective-permute-done.4
  174.1 1.5 collective-permute-done.5
  175.5 1.4 collective-permute-done.6
  177.0 5.1 %collective-permute-start.7 = (bf16[64,256]{1,0:T(8,128)(2,1)S(1)}, bf16[64,256]{1,0:T(8,128)(2,1)S(1)}, u32[]{:S(2)}, u32[]{:S(2)}) collective-permute-start(bf16[64,256]{1,0:T(8,128)(2,1)S(1)} %fusion.22), channel_id=1, source_target_pairs={{0,2},{1,3},{2,0},{3,1},{4,6},{5,7},{6,4},{7,5},{8,10},{9,11},{10,... | collective-permute-start | bytes 98312 | tf_op jit(solution)/shard_map/ppermute | solution.py:34
  182.1 1.6 collective-permute-done.7
  183.6 0.6 bitcast_add_fusion.1
  184.3 2.9 %all-to-all-done.6 = bf16[32,64,256]{2,1,0:T(8,128)(2,1)S(1)} async-done(((bf16[32,64,256]{2,1,0:T(8,128)(2,1)}), bf16[32,64,256]{2,1,0:T(8,128)(2,1)S(1)}, u32[]{:S(2)}, u32[]{:S(2)}) %all-to-all-start.6) | async-done | bytes 1048608 | tf_op jit(solution)/shard_map/all_to_all | solution.py:111
  187.1 0.8 convert_reduce_fusion
  (14 shorter events, 0.3 us)
Async XLA Ops:
  0.6 9.3 %copy-start = (bf16[256,2048]{1,0:T(8,128)(2,1)S(1)}, bf16[256,2048]{1,0:T(8,128)(2,1)}, u32[]{:S(2)}) copy-start(bf16[256,2048]{1,0:T(8,128)(2,1)} %param.7) | copy-start | bytes 3145732
  0.6 34.9 %copy-start.2 = (bf16[64,256]{1,0:T(8,128)(2,1)S(1)}, bf16[64,256]{1,0:T(8,128)(2,1)}, u32[]{:S(2)}) copy-start(bf16[64,256]{1,0:T(8,128)(2,1)} %param.10) | copy-start | bytes 98308
  2.2 17.1 %all-to-all-start = ((bf16[8,64,256]{2,1,0:T(8,128)(2,1)}), bf16[8,64,256]{2,1,0:T(8,128)(2,1)S(1)}, u32[]{:S(2)}, u32[]{:S(2)}) async-start(bf16[8,64,256]{2,1,0:T(8,128)(2,1)} %broadcast_in_dim.10), calls=%async_computation | async-start | bytes 524288 | tf_op jit(solution)/shard_map/all_to_all | solution.py:64
  12.0 52.1 %copy-start.4 = (bf16[8,2048]{1,0:T(8,128)(2,1)S(1)}, bf16[8,2048]{1,0:T(8,128)(2,1)}, u32[]{:S(2)}) copy-start(bf16[8,2048]{1,0:T(8,128)(2,1)} %param.9) | copy-start | bytes 98308
  19.3 44.7 %all-to-all-start.1 = ((bf16[32,8,2048]{2,1,0:T(8,128)(2,1)}), bf16[32,8,2048]{2,1,0:T(8,128)(2,1)S(1)}, u32[]{:S(2)}, u32[]{:S(2)}) async-start(bf16[32,8,2048]{2,1,0:T(8,128)(2,1)} %fusion.2), calls=%async_computation.1 | async-start | bytes 2097152 | tf_op jit(solution)/shard_map/all_to_all | solution.py:60
  25.9 37.8 %collective-permute-start = (bf16[8,64,256]{2,1,0:T(8,128)(2,1)S(1)}, bf16[8,64,256]{2,1,0:T(8,128)(2,1)S(1)}, u32[]{:S(2)}, u32[]{:S(2)}) collective-permute-start(bf16[8,64,256]{2,1,0:T(8,128)(2,1)S(1)} %all-to-all-done), channel_id=1, source_target_pairs={{0,16},{16,0},{32,48},{48,32},{64,80},{80,64},{96,112},{112,96},{1... | collective-permute-start | bytes 786440 | tf_op jit(solution)/shard_map/ppermute | solution.py:67
  29.0 34.7 %collective-permute-start.1 = (bf16[8,64,256]{2,1,0:T(8,128)(2,1)S(1)}, bf16[8,64,256]{2,1,0:T(8,128)(2,1)S(1)}, u32[]{:S(2)}, u32[]{:S(2)}) collective-permute-start(bf16[8,64,256]{2,1,0:T(8,128)(2,1)S(1)} %all-to-all-done), channel_id=1, source_target_pairs={{0,32},{16,48},{32,0},{48,16},{64,96},{80,112},{96,64},{112,80},{1... | collective-permute-start | bytes 786440 | tf_op jit(solution)/shard_map/ppermute | solution.py:67
  33.3 30.4 %collective-permute-start.2 = (bf16[8,64,256]{2,1,0:T(8,128)(2,1)S(1)}, bf16[8,64,256]{2,1,0:T(8,128)(2,1)S(1)}, u32[]{:S(2)}, u32[]{:S(2)}) collective-permute-start(bf16[8,64,256]{2,1,0:T(8,128)(2,1)S(1)} %all-to-all-done), channel_id=1, source_target_pairs={{0,48},{16,32},{32,16},{48,0},{64,112},{80,96},{96,80},{112,64},{1... | collective-permute-start | bytes 786440 | tf_op jit(solution)/shard_map/ppermute | solution.py:67
  65.3 36.4 %all-to-all-start.2 = ((bf16[32,8,2048]{2,1,0:T(8,128)(2,1)}), bf16[32,8,2048]{2,1,0:T(8,128)(2,1)}, u32[]{:S(2)}, u32[]{:S(2)}) async-start(bf16[32,8,2048]{2,1,0:T(8,128)(2,1)} %broadcast_in_dim.11), calls=%async_computation.2 | async-start | bytes 2097152 | tf_op jit(solution)/shard_map/all_to_all | solution.py:18
  77.1 3.1 %copy-start.3 = (bf16[16,1024]{1,0:T(8,128)(2,1)S(1)}, bf16[16,1024]{1,0:T(8,128)(2,1)}, u32[]{:S(2)}) copy-start(bf16[16,1024]{1,0:T(8,128)(2,1)} %param.8) | copy-start | bytes 98308
  134.4 12.9 %all-to-all-start.5 = ((f32[16,1,1024]{2,1,0:T(1,128)}), f32[16,1,1024]{2,1,0:T(1,128)S(1)}, u32[]{:S(2)}, u32[]{:S(2)}) async-start(f32[16,1,1024]{2,1,0:T(1,128)} %broadcast_in_dim.14), calls=%async_computation.5 | async-start | bytes 131072 | tf_op jit(solution)/shard_map/all_to_all | solution.py:18
  151.4 1.4 copy-start.1
  155.2 31.9 %all-to-all-start.6 = ((bf16[32,64,256]{2,1,0:T(8,128)(2,1)}), bf16[32,64,256]{2,1,0:T(8,128)(2,1)S(1)}, u32[]{:S(2)}, u32[]{:S(2)}) async-start(bf16[32,64,256]{2,1,0:T(8,128)(2,1)} %bitcast.93), calls=%async_computation.6 | async-start | bytes 2097152 | tf_op jit(solution)/shard_map/all_to_all | solution.py:111
  159.1 3.4 %collective-permute-start.3 = (bf16[8,64,256]{2,1,0:T(8,128)(2,1)S(1)}, bf16[8,64,256]{2,1,0:T(8,128)(2,1)S(1)}, u32[]{:S(2)}, u32[]{:S(2)}) collective-permute-start(bf16[8,64,256]{2,1,0:T(8,128)(2,1)S(1)} %fusion.9), channel_id=1, source_target_pairs={{0,1},{1,0},{2,3},{3,2},{4,5},{5,4},{6,7},{7,6},{8,9},{9,8},{10,11... | collective-permute-start | bytes 786440 | tf_op jit(solution)/shard_map/ppermute | solution.py:23
  162.7 11.4 %collective-permute-start.4 = (bf16[2,64,256]{2,1,0:T(8,128)(2,1)S(1)}, bf16[2,64,256]{2,1,0:T(8,128)(2,1)S(1)}, u32[]{:S(2)}, u32[]{:S(2)}) collective-permute-start(bf16[2,64,256]{2,1,0:T(8,128)(2,1)S(1)} %get-tuple-element.32), channel_id=1, source_target_pairs={{0,4},{1,5},{2,6},{3,7},{4,0},{5,1},{6,2},{7,3},{8,12},{9,13},{10,... | collective-permute-start | bytes 196616 | tf_op jit(solution)/shard_map/ppermute | solution.py:29
  164.9 10.7 %collective-permute-start.5 = (bf16[2,64,256]{2,1,0:T(8,128)(2,1)S(1)}, bf16[2,64,256]{2,1,0:T(8,128)(2,1)S(1)}, u32[]{:S(2)}, u32[]{:S(2)}) collective-permute-start(bf16[2,64,256]{2,1,0:T(8,128)(2,1)S(1)} %get-tuple-element.34), channel_id=1, source_target_pairs={{0,8},{1,9},{2,10},{3,11},{4,12},{5,13},{6,14},{7,15},{8,0},{9,1},... | collective-permute-start | bytes 196616 | tf_op jit(solution)/shard_map/ppermute | solution.py:29
  168.9 8.0 %collective-permute-start.6 = (bf16[2,64,256]{2,1,0:T(8,128)(2,1)S(1)}, bf16[2,64,256]{2,1,0:T(8,128)(2,1)S(1)}, u32[]{:S(2)}, u32[]{:S(2)}) collective-permute-start(bf16[2,64,256]{2,1,0:T(8,128)(2,1)S(1)} %get-tuple-element.33), channel_id=1, source_target_pairs={{0,12},{1,13},{2,14},{3,15},{4,8},{5,9},{6,10},{7,11},{8,4},{9,5},... | collective-permute-start | bytes 196616 | tf_op jit(solution)/shard_map/ppermute | solution.py:29
  177.0 6.7 %collective-permute-start.7 = (bf16[64,256]{1,0:T(8,128)(2,1)S(1)}, bf16[64,256]{1,0:T(8,128)(2,1)S(1)}, u32[]{:S(2)}, u32[]{:S(2)}) collective-permute-start(bf16[64,256]{1,0:T(8,128)(2,1)S(1)} %fusion.22), channel_id=1, source_target_pairs={{0,2},{1,3},{2,0},{3,1},{4,6},{5,7},{6,4},{7,5},{8,10},{9,11},{10,... | collective-permute-start | bytes 98312 | tf_op jit(solution)/shard_map/ppermute | solution.py:34

commit v5 on v4

--- a/solution.py
+++ b/solution.py
@@ -89,13 +89,14 @@
 
     reach = lax.dot_general(weighted, exp_block, (((1,), (1,)), ((), ())), preferred_element_type=F32)
     share = reach * (scale / row_sums)[None, :]
+    kept_share = share.astype(BF)
     norm_terms = jnp.sum(forward_all.astype(F32) * share, axis=1)
     norm_terms = jnp.sum(gather_by(norm_terms, "col", COLS), axis=0)
     norm_terms = jnp.sum(gather_by(norm_terms, "row", ROWS), axis=0)
     forward_all = forward_all.astype(F32)
     factor = jnp.float32(S) / jnp.float32(SEQS)
     coeffs = (factor * forward_all / (norm_terms[:, None] * row_sums[None, :])).astype(BF)
-    part = jnp.sum(coeffs.astype(F32) * share, axis=0)
+    part = jnp.sum(coeffs.astype(F32) * kept_share.astype(F32), axis=0)
     ratio = jnp.sum(gather_by(part, "col", COLS), axis=0)
 
     summed = lax.dot_general(coeffs, weighted, (((0,), (0,)), ((), ())), preferred_element_type=F32)

time: 189 us -> 187 us (0.989)
  no operation moved by 1% of the time
where the time goes in v5:
time: 187 us; the launch traced here: 186 us
  blocking collectives  70.7 us (38%)
  starting transfers between devices  60.7 us (32%)
  waiting for transfers between devices  27.9 us (15%)
  matrix products  16.1 us (9%)
  other arithmetic  5.91 us (3%)
  local copies, waits for them, and re-layouts  3.51 us (2%)
    all_gather x1, blocking collectives, on_device(): src_block = lax.all_gather(src_embed, 'col', axis=0, tiled=True)  28.2 us
    all_to_all x2, blocking collectives, gather_by(): return lax.all_to_all(jnp.broadcast_to(x[None], (n,) + x.shape), axis, 0, 0)  25.6 us
    all_gather x1, blocking collectives, on_device(): got = lax.all_gather(jnp.concatenate([forward_rows, local], axis=0), 'col')  16.9 us
    all_to_all x2, starting transfers between devices, gather_by(): return lax.all_to_all(jnp.broadcast_to(x[None], (n,) + x.shape), axis, 0, 0)  14.4 us
    all_to_all x2, waiting for transfers between devices, gather_by(): return lax.all_to_all(jnp.broadcast_to(x[None], (n,) + x.shape), axis, 0, 0)  12.1 us
    ppermute x3, starting transfers between devices, column_sum(): lax.ppermute(sent, 'col', [(k, k ^ 4 * d) for k in range(COLS)]).astype(F32)  11.4 us
    ppermute x3, starting transfers between devices, on_device(): lax.ppermute(held, 'row', [(k, k ^ d) for k in range(ROWS)])  9.58 us
    all_to_all x1, starting transfers between devices, on_device(): lax.all_to_all(jnp.broadcast_to(tgt_embed[None], (YS,) + tgt_embed.shape)...  7.65 us
  transfers between devices with their start and end apart: 13, of which 8 were waited for; matrix products, arithmetic and copies ran while one was open for 5% of the time, Pallas kernels for 0%

profile of v5, /device:TPU:1, one launch (start us, length us, event | category | flops | bytes accessed | tf_op | source)
XLA Modules:
  0.0 185.8 jit_solution(2529318157091170382)
XLA Ops:
  0.6 0.0 copy-start
  0.6 0.0 copy-start.2
  0.7 1.6 broadcast_in_dim.10
  2.2 7.7 %all-to-all-start = ((bf16[8,64,256]{2,1,0:T(8,128)(2,1)}), bf16[8,64,256]{2,1,0:T(8,128)(2,1)S(1)}, u32[]{:S(2)}, u32[]{:S(2)}) async-start(bf16[8,64,256]{2,1,0:T(8,128)(2,1)} %broadcast_in_dim.10), calls=%async_computation | async-start | bytes 524288 | tf_op jit(solution)/shard_map/all_to_all | solution.py:64
  9.9 0.0 copy-done
  9.9 2.1 %fusion.2 = bf16[32,8,2048]{2,1,0:T(8,128)(2,1)} fusion(bf16[256,2048]{1,0:T(8,128)(2,1)S(1)} %copy-done, s32[256]{0:T(256)S(1)} %iota_add_fusion, s32[256]{0:T(256)} %param.6), kind=kOutput, calls=%fused_computation.6 | convolution fusion | flops 269025280 | bytes 2099200 | tf_op jit(solution)/shard_map/dot_general | solution.py:57
  12.0 0.0 copy-start.4
  12.1 7.2 %all-to-all-done = bf16[8,64,256]{2,1,0:T(8,128)(2,1)S(1)} async-done(((bf16[8,64,256]{2,1,0:T(8,128)(2,1)}), bf16[8,64,256]{2,1,0:T(8,128)(2,1)S(1)}, u32[]{:S(2)}, u32[]{:S(2)}) %all-to-all-start) | async-done | bytes 262176 | tf_op jit(solution)/shard_map/all_to_all | solution.py:64
  19.3 6.6 %all-to-all-start.1 = ((bf16[32,8,2048]{2,1,0:T(8,128)(2,1)}), bf16[32,8,2048]{2,1,0:T(8,128)(2,1)S(1)}, u32[]{:S(2)}, u32[]{:S(2)}) async-start(bf16[32,8,2048]{2,1,0:T(8,128)(2,1)} %fusion.2), calls=%async_computation.1 | async-start | bytes 2097152 | tf_op jit(solution)/shard_map/all_to_all | solution.py:60
  25.9 3.1 %collective-permute-start = (bf16[8,64,256]{2,1,0:T(8,128)(2,1)S(1)}, bf16[8,64,256]{2,1,0:T(8,128)(2,1)S(1)}, u32[]{:S(2)}, u32[]{:S(2)}) collective-permute-start(bf16[8,64,256]{2,1,0:T(8,128)(2,1)S(1)} %all-to-all-done), channel_id=1, source_target_pairs={{0,16},{16,0},{32,48},{48,32},{64,80},{80,64},{96,112},{112,96},{1... | collective-permute-start | bytes 786440 | tf_op jit(solution)/shard_map/ppermute | solution.py:67
  29.0 4.3 %collective-permute-start.1 = (bf16[8,64,256]{2,1,0:T(8,128)(2,1)S(1)}, bf16[8,64,256]{2,1,0:T(8,128)(2,1)S(1)}, u32[]{:S(2)}, u32[]{:S(2)}) collective-permute-start(bf16[8,64,256]{2,1,0:T(8,128)(2,1)S(1)} %all-to-all-done), channel_id=1, source_target_pairs={{0,32},{16,48},{32,0},{48,16},{64,96},{80,112},{96,64},{112,80},{1... | collective-permute-start | bytes 786440 | tf_op jit(solution)/shard_map/ppermute | solution.py:67
  33.3 2.1 %collective-permute-start.2 = (bf16[8,64,256]{2,1,0:T(8,128)(2,1)S(1)}, bf16[8,64,256]{2,1,0:T(8,128)(2,1)S(1)}, u32[]{:S(2)}, u32[]{:S(2)}) collective-permute-start(bf16[8,64,256]{2,1,0:T(8,128)(2,1)S(1)} %all-to-all-done), channel_id=1, source_target_pairs={{0,48},{16,32},{32,16},{48,0},{64,112},{80,96},{96,80},{112,64},{1... | collective-permute-start | bytes 786440 | tf_op jit(solution)/shard_map/ppermute | solution.py:67
  35.5 0.0 copy-done.2
  35.5 28.2 %all_gather.9 = bf16[1024,256]{1,0:T(8,128)(2,1)} all-gather(bf16[64,256]{1,0:T(8,128)(2,1)S(1)} %copy-done.2), channel_id=1, replica_groups=mesh['row'=32,'col'=16] {'col'}, dimensions={0}, use_global_device_ids=true | all-gather | bytes 557056 | tf_op jit(solution)/shard_map/all_gather | solution.py:68
  63.7 0.0 collective-permute-done
  63.7 0.0 collective-permute-done.1
  63.7 0.0 collective-permute-done.2
  63.7 0.1 select_bitcast_fusion.3
  63.8 0.1 pad_maximum_fusion
  64.0 0.0 all-to-all-done.1
  64.0 0.2 convert_reduce_fusion.1
  64.1 0.0 copy-done.4
  64.2 1.1 broadcast_in_dim.11
  65.3 9.3 %all-to-all-start.2 = ((bf16[32,8,2048]{2,1,0:T(8,128)(2,1)}), bf16[32,8,2048]{2,1,0:T(8,128)(2,1)}, u32[]{:S(2)}, u32[]{:S(2)}) async-start(bf16[32,8,2048]{2,1,0:T(8,128)(2,1)} %broadcast_in_dim.11), calls=%async_computation.2 | async-start | bytes 2097152 | tf_op jit(solution)/shard_map/all_to_all | solution.py:18
  74.7 2.4 %fusion.26 = (f32[1024]{0:T(1024)S(1)}, f32[1024,2048]{1,0:T(8,128)S(1)}) fusion(bf16[1024,256]{1,0:T(8,128)(2,1)} %all_gather.9, bf16[2048,256]{1,0:T(8,128)(2,1)S(1)} %bitcast.84), kind=kOutput, calls=%fused_computation.67 | convolution fusion | flops 1075837952 | bytes 9965568 | tf_op jit(solution)/shard_map/dot_general | solution.py:74
  77.1 0.0 copy-start.3
  77.1 3.0 %fusion = (f32[1024]{0:T(1024)S(1)}, bf16[1024,2048]{1,0:T(8,128)(2,1)}) fusion(f32[1024,2048]{1,0:T(8,128)S(1)} %get-tuple-element.42, f32[1024]{0:T(1024)S(1)} %get-tuple-element.41), kind=kLoop, calls=%fused_computation.2 | loop fusion | flops 6290432 | bytes 12591104 | tf_op jit(solution)/shard_map/reduce_sum | solution.py:77
  80.1 0.0 copy-done.3
  80.2 16.9 %all-gather.1 = bf16[16,22,1024]{2,1,0:T(8,128)(2,1)S(1)} all-gather(bf16[1,22,1024]{2,1,0:T(8,128)(2,1)S(1)} %maximum_bitcast_fusion), channel_id=2, replica_groups=mesh['row'=32,'col'=16] {'col'}, dimensions={0}, use_global_device_ids=true | all-gather | bytes 765952 | tf_op jit(solution)/shard_map/all_gather | solution.py:82
  97.2 0.1 slice_add_fusion
  97.3 0.1 slice_reduce_fusion
  97.5 4.2 %all-to-all-done.2 = bf16[32,8,2048]{2,1,0:T(8,128)(2,1)} async-done(((bf16[32,8,2048]{2,1,0:T(8,128)(2,1)}), bf16[32,8,2048]{2,1,0:T(8,128)(2,1)}, u32[]{:S(2)}, u32[]{:S(2)}) %all-to-all-start.2) | async-done | bytes 1048608 | tf_op jit(solution)/shard_map/all_to_all | solution.py:18
  101.7 3.9 %fusion.5 = (f32[256]{0:T(256)S(1)}, bf16[256,1024]{1,0:T(8,128)(2,1)S(1)}) fusion(bf16[256,1024]{1,0:T(8,128)(2,1)S(1)} %bitcast.88, f32[1024]{0:T(1024)S(1)} %get-tuple-element.24, bf16[1024,2048]{1,0:T(8,128)(2,1)} %get-tuple-element.18, bf16[32,8,2048]{2,1,0:T(8,128)(2,1)} %all-to-all-done.2), kind=kOutput, calls=%fused_computation.14 | convolution fusion | flops 1075052288 | bytes 6296576 | tf_op jit(solution)/shard_map/dot_general | solution.py:90
  105.6 11.8 %all_to_all.38 = f32[16,1,256]{2,1,0:T(1,128)S(1)} all-to-all(f32[16,1,256]{2,1,0:T(1,128)S(1)} %broadcast_in_dim.12), channel_id=1, replica_groups=mesh['row'=32,'col'=16] {'col'}, dimensions={0} | all-to-all | bytes 32768 | tf_op jit(solution)/shard_map/all_to_all | solution.py:18
  117.5 13.8 %all_to_all.39 = f32[32,1,256]{2,1,0:T(1,128)S(1)} all-to-all(f32[32,1,256]{2,1,0:T(1,128)S(1)} %broadcast_in_dim.13), channel_id=1, replica_groups=mesh['row'=32,'col'=16] {'row'}, dimensions={0} | all-to-all | bytes 65536 | tf_op jit(solution)/shard_map/all_to_all | solution.py:18
  131.3 0.1 reduce_sum.86
  131.3 0.3 multiply_reduce_fusion
  131.7 0.7 broadcast_in_dim.14
  132.3 5.1 %all-to-all-start.5 = ((f32[16,1,1024]{2,1,0:T(1,128)}), f32[16,1,1024]{2,1,0:T(1,128)S(1)}, u32[]{:S(2)}, u32[]{:S(2)}) async-start(f32[16,1,1024]{2,1,0:T(1,128)} %broadcast_in_dim.14), calls=%async_computation.5 | async-start | bytes 131072 | tf_op jit(solution)/shard_map/all_to_all | solution.py:18
  137.4 7.8 %all-to-all-done.5 = f32[16,1,1024]{2,1,0:T(1,128)S(1)} async-done(((f32[16,1,1024]{2,1,0:T(1,128)}), f32[16,1,1024]{2,1,0:T(1,128)S(1)}, u32[]{:S(2)}, u32[]{:S(2)}) %all-to-all-start.5) | async-done | bytes 65568 | tf_op jit(solution)/shard_map/all_to_all | solution.py:18
  145.2 0.1 reduce_sum.88
  145.3 4.0 %multiply_convert_fusion = bf16[1024,2048]{1,0:T(8,128)(2,1)S(1)} fusion(bf16[1024,2048]{1,0:T(8,128)(2,1)} %get-tuple-element.18, f32[1024]{0:T(1024)S(1)} %reduce_sum.88, f32[1024]{0:T(1024)S(1)} %get-tuple-element.25, bf16[32,8,2048]{2,1,0:T(8,128)(2,1)} %all-to-all-done.2, bf16[256,1024]{1,0:T(8,128)(2,1)S(1)} %bitcast.90, f32[1024]{0:T(1024)S(1)} %fusion.21, ...), kind=kOutput, calls=%fused_computation | convolution fusion | flops 1085538304 | bytes 9974784 | tf_op jit(solution)/shard_map/dot_general | solution.py:102
  149.3 0.0 copy-start.1
  149.3 1.3 fusion.27
  150.6 0.1 fusion.8
  150.7 0.1 fusion.9
  150.7 0.0 copy-done.1
  150.7 2.4 %convolution_convert_fusion = bf16[2048,256]{1,0:T(8,128)(2,1)} fusion(bf16[1024,2048]{1,0:T(8,128)(2,1)S(1)} %multiply_convert_fusion, bf16[1024,256]{1,0:T(8,128)(2,1)S(1)} %copy-done.1), kind=kOutput, calls=%fused_computation.4 | convolution fusion | flops 1074266112 | bytes 5767168 | tf_op jit(solution)/shard_map/dot_general | solution.py:111
  153.1 3.9 %all-to-all-start.6 = ((bf16[32,64,256]{2,1,0:T(8,128)(2,1)}), bf16[32,64,256]{2,1,0:T(8,128)(2,1)S(1)}, u32[]{:S(2)}, u32[]{:S(2)}) async-start(bf16[32,64,256]{2,1,0:T(8,128)(2,1)} %bitcast.93), calls=%async_computation.6 | async-start | bytes 2097152 | tf_op jit(solution)/shard_map/all_to_all | solution.py:112
  157.1 2.1 %collective-permute-start.3 = (bf16[8,64,256]{2,1,0:T(8,128)(2,1)S(1)}, bf16[8,64,256]{2,1,0:T(8,128)(2,1)S(1)}, u32[]{:S(2)}, u32[]{:S(2)}) collective-permute-start(bf16[8,64,256]{2,1,0:T(8,128)(2,1)S(1)} %fusion.9), channel_id=1, source_target_pairs={{0,1},{1,0},{2,3},{3,2},{4,5},{5,4},{6,7},{7,6},{8,9},{9,8},{10,11... | collective-permute-start | bytes 786440 | tf_op jit(solution)/shard_map/ppermute | solution.py:23
  159.1 1.3 collective-permute-done.3
  160.5 0.1 convert_add_fusion
  160.6 2.2 %collective-permute-start.4 = (bf16[2,64,256]{2,1,0:T(8,128)(2,1)S(1)}, bf16[2,64,256]{2,1,0:T(8,128)(2,1)S(1)}, u32[]{:S(2)}, u32[]{:S(2)}) collective-permute-start(bf16[2,64,256]{2,1,0:T(8,128)(2,1)S(1)} %get-tuple-element.32), channel_id=1, source_target_pairs={{0,4},{1,5},{2,6},{3,7},{4,0},{5,1},{6,2},{7,3},{8,12},{9,13},{10,... | collective-permute-start | bytes 196616 | tf_op jit(solution)/shard_map/ppermute | solution.py:29
  162.8 4.0 %collective-permute-start.5 = (bf16[2,64,256]{2,1,0:T(8,128)(2,1)S(1)}, bf16[2,64,256]{2,1,0:T(8,128)(2,1)S(1)}, u32[]{:S(2)}, u32[]{:S(2)}) collective-permute-start(bf16[2,64,256]{2,1,0:T(8,128)(2,1)S(1)} %get-tuple-element.34), channel_id=1, source_target_pairs={{0,8},{1,9},{2,10},{3,11},{4,12},{5,13},{6,14},{7,15},{8,0},{9,1},... | collective-permute-start | bytes 196616 | tf_op jit(solution)/shard_map/ppermute | solution.py:29
  166.8 5.2 %collective-permute-start.6 = (bf16[2,64,256]{2,1,0:T(8,128)(2,1)S(1)}, bf16[2,64,256]{2,1,0:T(8,128)(2,1)S(1)}, u32[]{:S(2)}, u32[]{:S(2)}) collective-permute-start(bf16[2,64,256]{2,1,0:T(8,128)(2,1)S(1)} %get-tuple-element.33), channel_id=1, source_target_pairs={{0,12},{1,13},{2,14},{3,15},{4,8},{5,9},{6,10},{7,11},{8,4},{9,5},... | collective-permute-start | bytes 196616 | tf_op jit(solution)/shard_map/ppermute | solution.py:29
  172.0 0.0 collective-permute-done.4
  172.0 1.4 collective-permute-done.5
  173.4 1.3 collective-permute-done.6
  174.8 5.1 %collective-permute-start.7 = (bf16[64,256]{1,0:T(8,128)(2,1)S(1)}, bf16[64,256]{1,0:T(8,128)(2,1)S(1)}, u32[]{:S(2)}, u32[]{:S(2)}) collective-permute-start(bf16[64,256]{1,0:T(8,128)(2,1)S(1)} %fusion.22), channel_id=1, source_target_pairs={{0,2},{1,3},{2,0},{3,1},{4,6},{5,7},{6,4},{7,5},{8,10},{9,11},{10,... | collective-permute-start | bytes 98312 | tf_op jit(solution)/shard_map/ppermute | solution.py:34
  180.0 1.6 collective-permute-done.7
  181.5 0.6 bitcast_add_fusion.1
  182.2 2.9 %all-to-all-done.6 = bf16[32,64,256]{2,1,0:T(8,128)(2,1)S(1)} async-done(((bf16[32,64,256]{2,1,0:T(8,128)(2,1)}), bf16[32,64,256]{2,1,0:T(8,128)(2,1)S(1)}, u32[]{:S(2)}, u32[]{:S(2)}) %all-to-all-start.6) | async-done | bytes 1048608 | tf_op jit(solution)/shard_map/all_to_all | solution.py:112
  185.0 0.8 convert_reduce_fusion
  (14 shorter events, 0.3 us)
Async XLA Ops:
  0.6 9.3 %copy-start = (bf16[256,2048]{1,0:T(8,128)(2,1)S(1)}, bf16[256,2048]{1,0:T(8,128)(2,1)}, u32[]{:S(2)}) copy-start(bf16[256,2048]{1,0:T(8,128)(2,1)} %param.7) | copy-start | bytes 3145732
  0.6 34.9 %copy-start.2 = (bf16[64,256]{1,0:T(8,128)(2,1)S(1)}, bf16[64,256]{1,0:T(8,128)(2,1)}, u32[]{:S(2)}) copy-start(bf16[64,256]{1,0:T(8,128)(2,1)} %param.10) | copy-start | bytes 98308
  2.2 17.1 %all-to-all-start = ((bf16[8,64,256]{2,1,0:T(8,128)(2,1)}), bf16[8,64,256]{2,1,0:T(8,128)(2,1)S(1)}, u32[]{:S(2)}, u32[]{:S(2)}) async-start(bf16[8,64,256]{2,1,0:T(8,128)(2,1)} %broadcast_in_dim.10), calls=%async_computation | async-start | bytes 524288 | tf_op jit(solution)/shard_map/all_to_all | solution.py:64
  12.0 52.1 %copy-start.4 = (bf16[8,2048]{1,0:T(8,128)(2,1)S(1)}, bf16[8,2048]{1,0:T(8,128)(2,1)}, u32[]{:S(2)}) copy-start(bf16[8,2048]{1,0:T(8,128)(2,1)} %param.9) | copy-start | bytes 98308
  19.3 44.7 %all-to-all-start.1 = ((bf16[32,8,2048]{2,1,0:T(8,128)(2,1)}), bf16[32,8,2048]{2,1,0:T(8,128)(2,1)S(1)}, u32[]{:S(2)}, u32[]{:S(2)}) async-start(bf16[32,8,2048]{2,1,0:T(8,128)(2,1)} %fusion.2), calls=%async_computation.1 | async-start | bytes 2097152 | tf_op jit(solution)/shard_map/all_to_all | solution.py:60
  25.9 37.8 %collective-permute-start = (bf16[8,64,256]{2,1,0:T(8,128)(2,1)S(1)}, bf16[8,64,256]{2,1,0:T(8,128)(2,1)S(1)}, u32[]{:S(2)}, u32[]{:S(2)}) collective-permute-start(bf16[8,64,256]{2,1,0:T(8,128)(2,1)S(1)} %all-to-all-done), channel_id=1, source_target_pairs={{0,16},{16,0},{32,48},{48,32},{64,80},{80,64},{96,112},{112,96},{1... | collective-permute-start | bytes 786440 | tf_op jit(solution)/shard_map/ppermute | solution.py:67
  29.0 34.7 %collective-permute-start.1 = (bf16[8,64,256]{2,1,0:T(8,128)(2,1)S(1)}, bf16[8,64,256]{2,1,0:T(8,128)(2,1)S(1)}, u32[]{:S(2)}, u32[]{:S(2)}) collective-permute-start(bf16[8,64,256]{2,1,0:T(8,128)(2,1)S(1)} %all-to-all-done), channel_id=1, source_target_pairs={{0,32},{16,48},{32,0},{48,16},{64,96},{80,112},{96,64},{112,80},{1... | collective-permute-start | bytes 786440 | tf_op jit(solution)/shard_map/ppermute | solution.py:67
  33.3 30.4 %collective-permute-start.2 = (bf16[8,64,256]{2,1,0:T(8,128)(2,1)S(1)}, bf16[8,64,256]{2,1,0:T(8,128)(2,1)S(1)}, u32[]{:S(2)}, u32[]{:S(2)}) collective-permute-start(bf16[8,64,256]{2,1,0:T(8,128)(2,1)S(1)} %all-to-all-done), channel_id=1, source_target_pairs={{0,48},{16,32},{32,16},{48,0},{64,112},{80,96},{96,80},{112,64},{1... | collective-permute-start | bytes 786440 | tf_op jit(solution)/shard_map/ppermute | solution.py:67
  65.3 36.4 %all-to-all-start.2 = ((bf16[32,8,2048]{2,1,0:T(8,128)(2,1)}), bf16[32,8,2048]{2,1,0:T(8,128)(2,1)}, u32[]{:S(2)}, u32[]{:S(2)}) async-start(bf16[32,8,2048]{2,1,0:T(8,128)(2,1)} %broadcast_in_dim.11), calls=%async_computation.2 | async-start | bytes 2097152 | tf_op jit(solution)/shard_map/all_to_all | solution.py:18
  77.1 3.1 %copy-start.3 = (bf16[16,1024]{1,0:T(8,128)(2,1)S(1)}, bf16[16,1024]{1,0:T(8,128)(2,1)}, u32[]{:S(2)}) copy-start(bf16[16,1024]{1,0:T(8,128)(2,1)} %param.8) | copy-start | bytes 98308
  132.3 12.9 %all-to-all-start.5 = ((f32[16,1,1024]{2,1,0:T(1,128)}), f32[16,1,1024]{2,1,0:T(1,128)S(1)}, u32[]{:S(2)}, u32[]{:S(2)}) async-start(f32[16,1,1024]{2,1,0:T(1,128)} %broadcast_in_dim.14), calls=%async_computation.5 | async-start | bytes 131072 | tf_op jit(solution)/shard_map/all_to_all | solution.py:18
  149.3 1.4 copy-start.1
  153.1 31.9 %all-to-all-start.6 = ((bf16[32,64,256]{2,1,0:T(8,128)(2,1)}), bf16[32,64,256]{2,1,0:T(8,128)(2,1)S(1)}, u32[]{:S(2)}, u32[]{:S(2)}) async-start(bf16[32,64,256]{2,1,0:T(8,128)(2,1)} %bitcast.93), calls=%async_computation.6 | async-start | bytes 2097152 | tf_op jit(solution)/shard_map/all_to_all | solution.py:112
  157.1 3.4 %collective-permute-start.3 = (bf16[8,64,256]{2,1,0:T(8,128)(2,1)S(1)}, bf16[8,64,256]{2,1,0:T(8,128)(2,1)S(1)}, u32[]{:S(2)}, u32[]{:S(2)}) collective-permute-start(bf16[8,64,256]{2,1,0:T(8,128)(2,1)S(1)} %fusion.9), channel_id=1, source_target_pairs={{0,1},{1,0},{2,3},{3,2},{4,5},{5,4},{6,7},{7,6},{8,9},{9,8},{10,11... | collective-permute-start | bytes 786440 | tf_op jit(solution)/shard_map/ppermute | solution.py:23
  160.6 11.4 %collective-permute-start.4 = (bf16[2,64,256]{2,1,0:T(8,128)(2,1)S(1)}, bf16[2,64,256]{2,1,0:T(8,128)(2,1)S(1)}, u32[]{:S(2)}, u32[]{:S(2)}) collective-permute-start(bf16[2,64,256]{2,1,0:T(8,128)(2,1)S(1)} %get-tuple-element.32), channel_id=1, source_target_pairs={{0,4},{1,5},{2,6},{3,7},{4,0},{5,1},{6,2},{7,3},{8,12},{9,13},{10,... | collective-permute-start | bytes 196616 | tf_op jit(solution)/shard_map/ppermute | solution.py:29
  162.8 10.7 %collective-permute-start.5 = (bf16[2,64,256]{2,1,0:T(8,128)(2,1)S(1)}, bf16[2,64,256]{2,1,0:T(8,128)(2,1)S(1)}, u32[]{:S(2)}, u32[]{:S(2)}) collective-permute-start(bf16[2,64,256]{2,1,0:T(8,128)(2,1)S(1)} %get-tuple-element.34), channel_id=1, source_target_pairs={{0,8},{1,9},{2,10},{3,11},{4,12},{5,13},{6,14},{7,15},{8,0},{9,1},... | collective-permute-start | bytes 196616 | tf_op jit(solution)/shard_map/ppermute | solution.py:29
  166.8 8.0 %collective-permute-start.6 = (bf16[2,64,256]{2,1,0:T(8,128)(2,1)S(1)}, bf16[2,64,256]{2,1,0:T(8,128)(2,1)S(1)}, u32[]{:S(2)}, u32[]{:S(2)}) collective-permute-start(bf16[2,64,256]{2,1,0:T(8,128)(2,1)S(1)} %get-tuple-element.33), channel_id=1, source_target_pairs={{0,12},{1,13},{2,14},{3,15},{4,8},{5,9},{6,10},{7,11},{8,4},{9,5},... | collective-permute-start | bytes 196616 | tf_op jit(solution)/shard_map/ppermute | solution.py:29
  174.8 6.7 %collective-permute-start.7 = (bf16[64,256]{1,0:T(8,128)(2,1)S(1)}, bf16[64,256]{1,0:T(8,128)(2,1)S(1)}, u32[]{:S(2)}, u32[]{:S(2)}) collective-permute-start(bf16[64,256]{1,0:T(8,128)(2,1)S(1)} %fusion.22), channel_id=1, source_target_pairs={{0,2},{1,3},{2,0},{3,1},{4,6},{5,7},{6,4},{7,5},{8,10},{9,11},{10,... | collective-permute-start | bytes 98312 | tf_op jit(solution)/shard_map/ppermute | solution.py:34

commit v6 on v5

--- a/solution.py
+++ b/solution.py
@@ -97,6 +97,7 @@
     factor = jnp.float32(S) / jnp.float32(SEQS)
     coeffs = (factor * forward_all / (norm_terms[:, None] * row_sums[None, :])).astype(BF)
     part = jnp.sum(coeffs.astype(F32) * kept_share.astype(F32), axis=0)
+    coeffs, part = lax.optimization_barrier((coeffs, part))
     ratio = jnp.sum(gather_by(part, "col", COLS), axis=0)
 
     summed = lax.dot_general(coeffs, weighted, (((0,), (0,)), ((), ())), preferred_element_type=F32)

time: 187 us -> 188 us (level)
  no operation moved by 1% of the time
where the time goes in v6:
time: 188 us; the launch traced here: 187 us
  blocking collectives  70.7 us (38%)
  starting transfers between devices  60.7 us (32%)
  waiting for transfers between devices  27.9 us (15%)
  matrix products  16.6 us (9%)
  other arithmetic  6.97 us (4%)
  local copies, waits for them, and re-layouts  3.51 us (2%)
    all_gather x1, blocking collectives, on_device(): src_block = lax.all_gather(src_embed, 'col', axis=0, tiled=True)  28.2 us
    all_to_all x2, blocking collectives, gather_by(): return lax.all_to_all(jnp.broadcast_to(x[None], (n,) + x.shape), axis, 0, 0)  25.6 us
    all_gather x1, blocking collectives, on_device(): got = lax.all_gather(jnp.concatenate([forward_rows, local], axis=0), 'col')  16.9 us
    all_to_all x2, starting transfers between devices, gather_by(): return lax.all_to_all(jnp.broadcast_to(x[None], (n,) + x.shape), axis, 0, 0)  14.4 us
    all_to_all x2, waiting for transfers between devices, gather_by(): return lax.all_to_all(jnp.broadcast_to(x[None], (n,) + x.shape), axis, 0, 0)  12.1 us
    ppermute x3, starting transfers between devices, column_sum(): lax.ppermute(sent, 'col', [(k, k ^ 4 * d) for k in range(COLS)]).astype(F32)  11.4 us
    ppermute x3, starting transfers between devices, on_device(): lax.ppermute(held, 'row', [(k, k ^ d) for k in range(ROWS)])  9.58 us
    all_to_all x1, starting transfers between devices, on_device(): lax.all_to_all(jnp.broadcast_to(tgt_embed[None], (YS,) + tgt_embed.shape)...  7.65 us
  transfers between devices with their start and end apart: 13, of which 8 were waited for; matrix products, arithmetic and copies ran while one was open for 5% of the time, Pallas kernels for 0%

profile of v6, /device:TPU:1, one launch (start us, length us, event | category | flops | bytes accessed | tf_op | source)
XLA Modules:
  0.0 187.3 jit_solution(17727669890577115669)
XLA Ops:
  0.6 0.0 copy-start
  0.6 0.0 copy-start.2
  0.7 1.6 broadcast_in_dim.10
  2.2 7.7 %all-to-all-start = ((bf16[8,64,256]{2,1,0:T(8,128)(2,1)}), bf16[8,64,256]{2,1,0:T(8,128)(2,1)S(1)}, u32[]{:S(2)}, u32[]{:S(2)}) async-start(bf16[8,64,256]{2,1,0:T(8,128)(2,1)} %broadcast_in_dim.10), calls=%async_computation | async-start | bytes 524288 | tf_op jit(solution)/shard_map/all_to_all | solution.py:64
  9.9 0.0 copy-done
  9.9 2.1 %fusion.2 = bf16[32,8,2048]{2,1,0:T(8,128)(2,1)} fusion(bf16[256,2048]{1,0:T(8,128)(2,1)S(1)} %copy-done, s32[256]{0:T(256)S(1)} %iota_add_fusion, s32[256]{0:T(256)} %param.6), kind=kOutput, calls=%fused_computation.6 | convolution fusion | flops 269025280 | bytes 2099200 | tf_op jit(solution)/shard_map/dot_general | solution.py:57
  12.0 0.0 copy-start.4
  12.1 7.2 %all-to-all-done = bf16[8,64,256]{2,1,0:T(8,128)(2,1)S(1)} async-done(((bf16[8,64,256]{2,1,0:T(8,128)(2,1)}), bf16[8,64,256]{2,1,0:T(8,128)(2,1)S(1)}, u32[]{:S(2)}, u32[]{:S(2)}) %all-to-all-start) | async-done | bytes 262176 | tf_op jit(solution)/shard_map/all_to_all | solution.py:64
  19.3 6.6 %all-to-all-start.1 = ((bf16[32,8,2048]{2,1,0:T(8,128)(2,1)}), bf16[32,8,2048]{2,1,0:T(8,128)(2,1)S(1)}, u32[]{:S(2)}, u32[]{:S(2)}) async-start(bf16[32,8,2048]{2,1,0:T(8,128)(2,1)} %fusion.2), calls=%async_computation.1 | async-start | bytes 2097152 | tf_op jit(solution)/shard_map/all_to_all | solution.py:60
  25.9 3.1 %collective-permute-start = (bf16[8,64,256]{2,1,0:T(8,128)(2,1)S(1)}, bf16[8,64,256]{2,1,0:T(8,128)(2,1)S(1)}, u32[]{:S(2)}, u32[]{:S(2)}) collective-permute-start(bf16[8,64,256]{2,1,0:T(8,128)(2,1)S(1)} %all-to-all-done), channel_id=1, source_target_pairs={{0,16},{16,0},{32,48},{48,32},{64,80},{80,64},{96,112},{112,96},{1... | collective-permute-start | bytes 786440 | tf_op jit(solution)/shard_map/ppermute | solution.py:67
  29.0 4.3 %collective-permute-start.1 = (bf16[8,64,256]{2,1,0:T(8,128)(2,1)S(1)}, bf16[8,64,256]{2,1,0:T(8,128)(2,1)S(1)}, u32[]{:S(2)}, u32[]{:S(2)}) collective-permute-start(bf16[8,64,256]{2,1,0:T(8,128)(2,1)S(1)} %all-to-all-done), channel_id=1, source_target_pairs={{0,32},{16,48},{32,0},{48,16},{64,96},{80,112},{96,64},{112,80},{1... | collective-permute-start | bytes 786440 | tf_op jit(solution)/shard_map/ppermute | solution.py:67
  33.3 2.1 %collective-permute-start.2 = (bf16[8,64,256]{2,1,0:T(8,128)(2,1)S(1)}, bf16[8,64,256]{2,1,0:T(8,128)(2,1)S(1)}, u32[]{:S(2)}, u32[]{:S(2)}) collective-permute-start(bf16[8,64,256]{2,1,0:T(8,128)(2,1)S(1)} %all-to-all-done), channel_id=1, source_target_pairs={{0,48},{16,32},{32,16},{48,0},{64,112},{80,96},{96,80},{112,64},{1... | collective-permute-start | bytes 786440 | tf_op jit(solution)/shard_map/ppermute | solution.py:67
  35.5 0.0 copy-done.2
  35.5 28.2 %all_gather.9 = bf16[1024,256]{1,0:T(8,128)(2,1)} all-gather(bf16[64,256]{1,0:T(8,128)(2,1)S(1)} %copy-done.2), channel_id=1, replica_groups=mesh['row'=32,'col'=16] {'col'}, dimensions={0}, use_global_device_ids=true | all-gather | bytes 557056 | tf_op jit(solution)/shard_map/all_gather | solution.py:68
  63.7 0.0 collective-permute-done
  63.7 0.0 collective-permute-done.1
  63.7 0.0 collective-permute-done.2
  63.7 0.1 select_bitcast_fusion.3
  63.8 0.1 pad_maximum_fusion
  64.0 0.0 all-to-all-done.1
  64.0 0.2 convert_reduce_fusion.1
  64.1 0.0 copy-done.4
  64.2 1.1 broadcast_in_dim.11
  65.3 9.3 %all-to-all-start.2 = ((bf16[32,8,2048]{2,1,0:T(8,128)(2,1)}), bf16[32,8,2048]{2,1,0:T(8,128)(2,1)}, u32[]{:S(2)}, u32[]{:S(2)}) async-start(bf16[32,8,2048]{2,1,0:T(8,128)(2,1)} %broadcast_in_dim.11), calls=%async_computation.2 | async-start | bytes 2097152 | tf_op jit(solution)/shard_map/all_to_all | solution.py:18
  74.7 2.4 %fusion.26 = (f32[1024]{0:T(1024)S(1)}, f32[1024,2048]{1,0:T(8,128)S(1)}) fusion(bf16[1024,256]{1,0:T(8,128)(2,1)} %all_gather.9, bf16[2048,256]{1,0:T(8,128)(2,1)S(1)} %bitcast.85), kind=kOutput, calls=%fused_computation.67 | convolution fusion | flops 1075837952 | bytes 9965568 | tf_op jit(solution)/shard_map/dot_general | solution.py:74
  77.1 0.0 copy-start.3
  77.1 3.0 %fusion = (f32[1024]{0:T(1024)S(1)}, bf16[1024,2048]{1,0:T(8,128)(2,1)}) fusion(f32[1024,2048]{1,0:T(8,128)S(1)} %get-tuple-element.48, f32[1024]{0:T(1024)S(1)} %get-tuple-element.47), kind=kLoop, calls=%fused_computation.2 | loop fusion | flops 6290432 | bytes 12591104 | tf_op jit(solution)/shard_map/reduce_sum | solution.py:77
  80.1 0.0 copy-done.3
  80.2 16.9 %all-gather.1 = bf16[16,22,1024]{2,1,0:T(8,128)(2,1)S(1)} all-gather(bf16[1,22,1024]{2,1,0:T(8,128)(2,1)S(1)} %maximum_bitcast_fusion), channel_id=2, replica_groups=mesh['row'=32,'col'=16] {'col'}, dimensions={0}, use_global_device_ids=true | all-gather | bytes 765952 | tf_op jit(solution)/shard_map/all_gather | solution.py:82
  97.2 0.1 slice_add_fusion
  97.3 0.1 slice_reduce_fusion
  97.5 4.2 %all-to-all-done.2 = bf16[32,8,2048]{2,1,0:T(8,128)(2,1)} async-done(((bf16[32,8,2048]{2,1,0:T(8,128)(2,1)}), bf16[32,8,2048]{2,1,0:T(8,128)(2,1)}, u32[]{:S(2)}, u32[]{:S(2)}) %all-to-all-start.2) | async-done | bytes 1048608 | tf_op jit(solution)/shard_map/all_to_all | solution.py:18
  101.7 4.6 %fusion.5 = (f32[256]{0:T(256)S(1)}, bf16[256,1024]{1,0:T(8,128)(2,1)}) fusion(bf16[256,1024]{1,0:T(8,128)(2,1)S(1)} %bitcast.89, f32[1024]{0:T(1024)S(1)} %get-tuple-element.30, bf16[1024,2048]{1,0:T(8,128)(2,1)} %get-tuple-element.20, bf16[32,8,2048]{2,1,0:T(8,128)(2,1)} %all-to-all-done.2), kind=kOutput, calls=%fused_computation.14 | convolution fusion | flops 1075052288 | bytes 6296576 | tf_op jit(solution)/shard_map/dot_general | solution.py:90
  106.4 11.8 %all_to_all.38 = f32[16,1,256]{2,1,0:T(1,128)S(1)} all-to-all(f32[16,1,256]{2,1,0:T(1,128)S(1)} %broadcast_in_dim.12), channel_id=1, replica_groups=mesh['row'=32,'col'=16] {'col'}, dimensions={0} | all-to-all | bytes 32768 | tf_op jit(solution)/shard_map/all_to_all | solution.py:18
  118.2 13.8 %all_to_all.39 = f32[32,1,256]{2,1,0:T(1,128)S(1)} all-to-all(f32[32,1,256]{2,1,0:T(1,128)S(1)} %broadcast_in_dim.13), channel_id=1, replica_groups=mesh['row'=32,'col'=16] {'row'}, dimensions={0} | all-to-all | bytes 65536 | tf_op jit(solution)/shard_map/all_to_all | solution.py:18
  132.0 0.1 reduce_sum.86
  132.0 1.4 multiply_reduce_fusion
  133.4 0.7 broadcast_in_dim.14
  134.1 5.1 %all-to-all-start.5 = ((f32[16,1,1024]{2,1,0:T(1,128)}), f32[16,1,1024]{2,1,0:T(1,128)S(1)}, u32[]{:S(2)}, u32[]{:S(2)}) async-start(f32[16,1,1024]{2,1,0:T(1,128)} %broadcast_in_dim.14), calls=%async_computation.5 | async-start | bytes 131072 | tf_op jit(solution)/shard_map/all_to_all | solution.py:18
  139.2 7.8 %all-to-all-done.5 = f32[16,1,1024]{2,1,0:T(1,128)S(1)} async-done(((f32[16,1,1024]{2,1,0:T(1,128)}), f32[16,1,1024]{2,1,0:T(1,128)S(1)}, u32[]{:S(2)}, u32[]{:S(2)}) %all-to-all-start.5) | async-done | bytes 65568 | tf_op jit(solution)/shard_map/all_to_all | solution.py:18
  147.0 0.1 reduce_sum.88
  147.1 3.8 %multiply_convert_fusion = bf16[1024,2048]{1,0:T(8,128)(2,1)S(1)} fusion(bf16[1024,2048]{1,0:T(8,128)(2,1)} %get-tuple-element.20, bf16[256,1024]{1,0:T(8,128)(2,1)S(1)} %get-tuple-element.23, f32[1024]{0:T(1024)S(1)} %reduce_sum.88, f32[1024]{0:T(1024)S(1)} %get-tuple-element.31, bf16[32,8,2048]{2,1,0:T(8,128)(2,1)} %all-to-all-done.2), kind=kOutput, calls=%fused_computation | convolution fusion | flops 1084227584 | bytes 9969664 | tf_op jit(solution)/shard_map/dot_general | solution.py:103
  150.9 0.0 copy-start.1
  150.9 1.3 fusion.27
  152.1 0.1 fusion.8
  152.2 0.1 fusion.9
  152.3 0.0 copy-done.1
  152.3 2.4 %convolution_convert_fusion = bf16[2048,256]{1,0:T(8,128)(2,1)} fusion(bf16[1024,2048]{1,0:T(8,128)(2,1)S(1)} %multiply_convert_fusion, bf16[1024,256]{1,0:T(8,128)(2,1)S(1)} %copy-done.1), kind=kOutput, calls=%fused_computation.4 | convolution fusion | flops 1074266112 | bytes 5767168 | tf_op jit(solution)/shard_map/dot_general | solution.py:112
  154.6 3.9 %all-to-all-start.6 = ((bf16[32,64,256]{2,1,0:T(8,128)(2,1)}), bf16[32,64,256]{2,1,0:T(8,128)(2,1)S(1)}, u32[]{:S(2)}, u32[]{:S(2)}) async-start(bf16[32,64,256]{2,1,0:T(8,128)(2,1)} %bitcast.93), calls=%async_computation.6 | async-start | bytes 2097152 | tf_op jit(solution)/shard_map/all_to_all | solution.py:113
  158.6 2.1 %collective-permute-start.3 = (bf16[8,64,256]{2,1,0:T(8,128)(2,1)S(1)}, bf16[8,64,256]{2,1,0:T(8,128)(2,1)S(1)}, u32[]{:S(2)}, u32[]{:S(2)}) collective-permute-start(bf16[8,64,256]{2,1,0:T(8,128)(2,1)S(1)} %fusion.9), channel_id=1, source_target_pairs={{0,1},{1,0},{2,3},{3,2},{4,5},{5,4},{6,7},{7,6},{8,9},{9,8},{10,11... | collective-permute-start | bytes 786440 | tf_op jit(solution)/shard_map/ppermute | solution.py:23
  160.7 1.3 collective-permute-done.3
  162.0 0.1 convert_add_fusion
  162.1 2.2 %collective-permute-start.4 = (bf16[2,64,256]{2,1,0:T(8,128)(2,1)S(1)}, bf16[2,64,256]{2,1,0:T(8,128)(2,1)S(1)}, u32[]{:S(2)}, u32[]{:S(2)}) collective-permute-start(bf16[2,64,256]{2,1,0:T(8,128)(2,1)S(1)} %get-tuple-element.38), channel_id=1, source_target_pairs={{0,4},{1,5},{2,6},{3,7},{4,0},{5,1},{6,2},{7,3},{8,12},{9,13},{10,... | collective-permute-start | bytes 196616 | tf_op jit(solution)/shard_map/ppermute | solution.py:29
  164.3 4.0 %collective-permute-start.5 = (bf16[2,64,256]{2,1,0:T(8,128)(2,1)S(1)}, bf16[2,64,256]{2,1,0:T(8,128)(2,1)S(1)}, u32[]{:S(2)}, u32[]{:S(2)}) collective-permute-start(bf16[2,64,256]{2,1,0:T(8,128)(2,1)S(1)} %get-tuple-element.40), channel_id=1, source_target_pairs={{0,8},{1,9},{2,10},{3,11},{4,12},{5,13},{6,14},{7,15},{8,0},{9,1},... | collective-permute-start | bytes 196616 | tf_op jit(solution)/shard_map/ppermute | solution.py:29
  168.3 5.2 %collective-permute-start.6 = (bf16[2,64,256]{2,1,0:T(8,128)(2,1)S(1)}, bf16[2,64,256]{2,1,0:T(8,128)(2,1)S(1)}, u32[]{:S(2)}, u32[]{:S(2)}) collective-permute-start(bf16[2,64,256]{2,1,0:T(8,128)(2,1)S(1)} %get-tuple-element.39), channel_id=1, source_target_pairs={{0,12},{1,13},{2,14},{3,15},{4,8},{5,9},{6,10},{7,11},{8,4},{9,5},... | collective-permute-start | bytes 196616 | tf_op jit(solution)/shard_map/ppermute | solution.py:29
  173.5 0.0 collective-permute-done.4
  173.5 1.5 collective-permute-done.5
  175.0 1.3 collective-permute-done.6
  176.4 5.1 %collective-permute-start.7 = (bf16[64,256]{1,0:T(8,128)(2,1)S(1)}, bf16[64,256]{1,0:T(8,128)(2,1)S(1)}, u32[]{:S(2)}, u32[]{:S(2)}) collective-permute-start(bf16[64,256]{1,0:T(8,128)(2,1)S(1)} %fusion.22), channel_id=1, source_target_pairs={{0,2},{1,3},{2,0},{3,1},{4,6},{5,7},{6,4},{7,5},{8,10},{9,11},{10,... | collective-permute-start | bytes 98312 | tf_op jit(solution)/shard_map/ppermute | solution.py:34
  181.5 1.6 collective-permute-done.7
  183.1 0.6 bitcast_add_fusion.1
  183.7 2.8 %all-to-all-done.6 = bf16[32,64,256]{2,1,0:T(8,128)(2,1)S(1)} async-done(((bf16[32,64,256]{2,1,0:T(8,128)(2,1)}), bf16[32,64,256]{2,1,0:T(8,128)(2,1)S(1)}, u32[]{:S(2)}, u32[]{:S(2)}) %all-to-all-start.6) | async-done | bytes 1048608 | tf_op jit(solution)/shard_map/all_to_all | solution.py:113
  186.6 0.8 convert_reduce_fusion
  (14 shorter events, 0.3 us)
Async XLA Ops:
  0.6 9.3 %copy-start = (bf16[256,2048]{1,0:T(8,128)(2,1)S(1)}, bf16[256,2048]{1,0:T(8,128)(2,1)}, u32[]{:S(2)}) copy-start(bf16[256,2048]{1,0:T(8,128)(2,1)} %param.7) | copy-start | bytes 3145732
  0.6 34.9 %copy-start.2 = (bf16[64,256]{1,0:T(8,128)(2,1)S(1)}, bf16[64,256]{1,0:T(8,128)(2,1)}, u32[]{:S(2)}) copy-start(bf16[64,256]{1,0:T(8,128)(2,1)} %param.10) | copy-start | bytes 98308
  2.2 17.1 %all-to-all-start = ((bf16[8,64,256]{2,1,0:T(8,128)(2,1)}), bf16[8,64,256]{2,1,0:T(8,128)(2,1)S(1)}, u32[]{:S(2)}, u32[]{:S(2)}) async-start(bf16[8,64,256]{2,1,0:T(8,128)(2,1)} %broadcast_in_dim.10), calls=%async_computation | async-start | bytes 524288 | tf_op jit(solution)/shard_map/all_to_all | solution.py:64
  12.0 52.1 %copy-start.4 = (bf16[8,2048]{1,0:T(8,128)(2,1)S(1)}, bf16[8,2048]{1,0:T(8,128)(2,1)}, u32[]{:S(2)}) copy-start(bf16[8,2048]{1,0:T(8,128)(2,1)} %param.9) | copy-start | bytes 98308
  19.3 44.7 %all-to-all-start.1 = ((bf16[32,8,2048]{2,1,0:T(8,128)(2,1)}), bf16[32,8,2048]{2,1,0:T(8,128)(2,1)S(1)}, u32[]{:S(2)}, u32[]{:S(2)}) async-start(bf16[32,8,2048]{2,1,0:T(8,128)(2,1)} %fusion.2), calls=%async_computation.1 | async-start | bytes 2097152 | tf_op jit(solution)/shard_map/all_to_all | solution.py:60
  25.9 37.8 %collective-permute-start = (bf16[8,64,256]{2,1,0:T(8,128)(2,1)S(1)}, bf16[8,64,256]{2,1,0:T(8,128)(2,1)S(1)}, u32[]{:S(2)}, u32[]{:S(2)}) collective-permute-start(bf16[8,64,256]{2,1,0:T(8,128)(2,1)S(1)} %all-to-all-done), channel_id=1, source_target_pairs={{0,16},{16,0},{32,48},{48,32},{64,80},{80,64},{96,112},{112,96},{1... | collective-permute-start | bytes 786440 | tf_op jit(solution)/shard_map/ppermute | solution.py:67
  29.0 34.7 %collective-permute-start.1 = (bf16[8,64,256]{2,1,0:T(8,128)(2,1)S(1)}, bf16[8,64,256]{2,1,0:T(8,128)(2,1)S(1)}, u32[]{:S(2)}, u32[]{:S(2)}) collective-permute-start(bf16[8,64,256]{2,1,0:T(8,128)(2,1)S(1)} %all-to-all-done), channel_id=1, source_target_pairs={{0,32},{16,48},{32,0},{48,16},{64,96},{80,112},{96,64},{112,80},{1... | collective-permute-start | bytes 786440 | tf_op jit(solution)/shard_map/ppermute | solution.py:67
  33.3 30.4 %collective-permute-start.2 = (bf16[8,64,256]{2,1,0:T(8,128)(2,1)S(1)}, bf16[8,64,256]{2,1,0:T(8,128)(2,1)S(1)}, u32[]{:S(2)}, u32[]{:S(2)}) collective-permute-start(bf16[8,64,256]{2,1,0:T(8,128)(2,1)S(1)} %all-to-all-done), channel_id=1, source_target_pairs={{0,48},{16,32},{32,16},{48,0},{64,112},{80,96},{96,80},{112,64},{1... | collective-permute-start | bytes 786440 | tf_op jit(solution)/shard_map/ppermute | solution.py:67
  65.3 36.4 %all-to-all-start.2 = ((bf16[32,8,2048]{2,1,0:T(8,128)(2,1)}), bf16[32,8,2048]{2,1,0:T(8,128)(2,1)}, u32[]{:S(2)}, u32[]{:S(2)}) async-start(bf16[32,8,2048]{2,1,0:T(8,128)(2,1)} %broadcast_in_dim.11), calls=%async_computation.2 | async-start | bytes 2097152 | tf_op jit(solution)/shard_map/all_to_all | solution.py:18
  77.1 3.1 %copy-start.3 = (bf16[16,1024]{1,0:T(8,128)(2,1)S(1)}, bf16[16,1024]{1,0:T(8,128)(2,1)}, u32[]{:S(2)}) copy-start(bf16[16,1024]{1,0:T(8,128)(2,1)} %param.8) | copy-start | bytes 98308
  134.1 12.9 %all-to-all-start.5 = ((f32[16,1,1024]{2,1,0:T(1,128)}), f32[16,1,1024]{2,1,0:T(1,128)S(1)}, u32[]{:S(2)}, u32[]{:S(2)}) async-start(f32[16,1,1024]{2,1,0:T(1,128)} %broadcast_in_dim.14), calls=%async_computation.5 | async-start | bytes 131072 | tf_op jit(solution)/shard_map/all_to_all | solution.py:18
  150.9 1.4 copy-start.1
  154.6 31.9 %all-to-all-start.6 = ((bf16[32,64,256]{2,1,0:T(8,128)(2,1)}), bf16[32,64,256]{2,1,0:T(8,128)(2,1)S(1)}, u32[]{:S(2)}, u32[]{:S(2)}) async-start(bf16[32,64,256]{2,1,0:T(8,128)(2,1)} %bitcast.93), calls=%async_computation.6 | async-start | bytes 2097152 | tf_op jit(solution)/shard_map/all_to_all | solution.py:113
  158.6 3.4 %collective-permute-start.3 = (bf16[8,64,256]{2,1,0:T(8,128)(2,1)S(1)}, bf16[8,64,256]{2,1,0:T(8,128)(2,1)S(1)}, u32[]{:S(2)}, u32[]{:S(2)}) collective-permute-start(bf16[8,64,256]{2,1,0:T(8,128)(2,1)S(1)} %fusion.9), channel_id=1, source_target_pairs={{0,1},{1,0},{2,3},{3,2},{4,5},{5,4},{6,7},{7,6},{8,9},{9,8},{10,11... | collective-permute-start | bytes 786440 | tf_op jit(solution)/shard_map/ppermute | solution.py:23
  162.1 11.4 %collective-permute-start.4 = (bf16[2,64,256]{2,1,0:T(8,128)(2,1)S(1)}, bf16[2,64,256]{2,1,0:T(8,128)(2,1)S(1)}, u32[]{:S(2)}, u32[]{:S(2)}) collective-permute-start(bf16[2,64,256]{2,1,0:T(8,128)(2,1)S(1)} %get-tuple-element.38), channel_id=1, source_target_pairs={{0,4},{1,5},{2,6},{3,7},{4,0},{5,1},{6,2},{7,3},{8,12},{9,13},{10,... | collective-permute-start | bytes 196616 | tf_op jit(solution)/shard_map/ppermute | solution.py:29
  164.3 10.7 %collective-permute-start.5 = (bf16[2,64,256]{2,1,0:T(8,128)(2,1)S(1)}, bf16[2,64,256]{2,1,0:T(8,128)(2,1)S(1)}, u32[]{:S(2)}, u32[]{:S(2)}) collective-permute-start(bf16[2,64,256]{2,1,0:T(8,128)(2,1)S(1)} %get-tuple-element.40), channel_id=1, source_target_pairs={{0,8},{1,9},{2,10},{3,11},{4,12},{5,13},{6,14},{7,15},{8,0},{9,1},... | collective-permute-start | bytes 196616 | tf_op jit(solution)/shard_map/ppermute | solution.py:29
  168.3 8.0 %collective-permute-start.6 = (bf16[2,64,256]{2,1,0:T(8,128)(2,1)S(1)}, bf16[2,64,256]{2,1,0:T(8,128)(2,1)S(1)}, u32[]{:S(2)}, u32[]{:S(2)}) collective-permute-start(bf16[2,64,256]{2,1,0:T(8,128)(2,1)S(1)} %get-tuple-element.39), channel_id=1, source_target_pairs={{0,12},{1,13},{2,14},{3,15},{4,8},{5,9},{6,10},{7,11},{8,4},{9,5},... | collective-permute-start | bytes 196616 | tf_op jit(solution)/shard_map/ppermute | solution.py:29
  176.4 6.7 %collective-permute-start.7 = (bf16[64,256]{1,0:T(8,128)(2,1)S(1)}, bf16[64,256]{1,0:T(8,128)(2,1)S(1)}, u32[]{:S(2)}, u32[]{:S(2)}) collective-permute-start(bf16[64,256]{1,0:T(8,128)(2,1)S(1)} %fusion.22), channel_id=1, source_target_pairs={{0,2},{1,3},{2,0},{3,1},{4,6},{5,7},{6,4},{7,5},{8,10},{9,11},{10,... | collective-permute-start | bytes 98312 | tf_op jit(solution)/shard_map/ppermute | solution.py:34
